TPU v7x, 128 devices: a whole 4x4x4 slice. The times are simulated.
128 devices in a mesh: seq: 32 (over y, x, core), exp: 4 (over z).
Axes of the slice: x: 4, y: 4, z: 4, core: 2. Of those that a mesh axis runs over, the one named last changes fastest.
Arguments:
- queries: bfloat16 [16384, 4096], P('seq', 'exp'), may hold values from -200 to 200
- keys: bfloat16 [16384, 512], P('seq', 'exp'), may hold values from -8 to 8
- values: bfloat16 [16384, 512], P('seq', 'exp'), may hold values from -6 to 6
- doc_lengths: int32 [16], replicated, may hold values from 1 to 2048, 16384 in all
- out_weight: bfloat16 [4096, 4096], P('exp', 'seq'), may hold values from -0.09375 to 0.09375
- residual: bfloat16 [16384, 4096], P(('seq', 'exp')), may hold values from -3 to 3
- norm_gain: float32 [4096], replicated, may hold values from 0.5 to 1.5
- expert_ids: int32 [16384, 8], P(('seq', 'exp')), may hold values from 0 to 127, all different within a row; in each aligned block of 128 rows (0 to 127, 128 to 255, ...) at most 9 rows name the same one
- gate_values: float32 [16384, 8], P(('seq', 'exp')), may hold values from 0.05 to 0.3
- w_gate: bfloat16 [128, 4096, 768], P(('seq', 'exp')), may hold values from -0.09375 to 0.09375
- w_up: bfloat16 [128, 4096, 768], P(('seq', 'exp')), may hold values from -0.09375 to 0.09375
- w_down: bfloat16 [128, 768, 4096], P(('seq', 'exp')), may hold values from -0.21875 to 0.21875
Outputs:
- mixed: bfloat16 [16384, 4096], P(('seq', 'exp'))
Inputs may be any that keep to these rules, and one draw needn't show every extreme that they name: `doc_lengths`: the 16 documents fill the row of 16384 tokens in order; the longest has exactly 2048 tokens. `expert_ids`: among the routes of one device's 128 tokens (aligned blocks of tokens in order), no expert is named more than 9 times, a bound that some block reaches; a token names 8 different experts.
All inputs are finite; a program needn't handle non-finite values.
Results may differ from a plain program's by a relative error of at most 0.015.
Values may be sent and summed in bfloat16 or wider, within the bound.
A program may use at most 192 MiB of HBM per device.

v0:
```python
import jax
import jax.numpy as jnp
from jax import lax
from jax.sharding import PartitionSpec as P

HEAD_DIM = 128
DOC_SHARDS = 4


NEG_FILL = -1e30


def passed_along(x, axis, by):
    count = lax.axis_size(axis)
    pairs = [(i, i + by) for i in range(count) if 0 <= i + by < count]
    return lax.ppermute(x, axis, pairs)


def doc_index(positions, doc_ends):
    return jnp.sum((positions[:, None] >= doc_ends[None, :]).astype(jnp.int32), axis=1)


def body(
    queries,
    keys,
    values,
    doc_lengths,
    out_weight,
    residual,
    norm_gain,
    expert_ids,
    gate_values,
    w_gate,
    w_up,
    w_down,
):
    row_count = queries.shape[0]
    kv_local = keys.shape[1] // HEAD_DIM
    group = queries.shape[1] // keys.shape[1]
    scale = HEAD_DIM ** (-0.5)
    doc_ends = jnp.cumsum(doc_lengths)
    my_start = lax.axis_index("seq") * row_count
    query_pos = my_start + jnp.arange(row_count, dtype=jnp.int32)
    query_doc = doc_index(query_pos, doc_ends)
    query_heads = queries.reshape(row_count, kv_local, group, HEAD_DIM)

    def attend_part(running, key_part, value_part, first):
        width = key_part.shape[0]
        key_pos = first + jnp.arange(width, dtype=jnp.int32)
        key_doc = doc_index(key_pos, doc_ends)
        visible = (
            (key_pos[None, :] >= 0)
            & (key_pos[None, :] <= query_pos[:, None])
            & (key_doc[None, :] == query_doc[:, None])
        )

        def update(state):
            top_old, total_old, accum_old = state
            scores = (
                jnp.einsum(
                    "tkgd,skd->kgts",
                    query_heads,
                    key_part.reshape(width, kv_local, HEAD_DIM),
                    preferred_element_type=jnp.float32,
                )
                * scale
            )
            masked = jnp.where(visible, scores, NEG_FILL)
            top_new = jnp.maximum(top_old, jnp.max(masked, axis=-1))
            factor = jnp.exp(top_old - top_new)
            weights = jnp.where(visible, jnp.exp(masked - top_new[..., None]), 0.0)
            total_new = total_old * factor + jnp.sum(weights, axis=-1)
            added = jnp.einsum(
                "kgts,skd->kgtd",
                weights.astype(jnp.bfloat16),
                value_part.reshape(width, kv_local, HEAD_DIM),
                preferred_element_type=jnp.float32,
            )
            return (top_new, total_new, accum_old * factor[..., None] + added)

        return lax.cond(jnp.any(visible), update, lambda state: state, running)

    def absorb(running, shards, offset):
        key_all, value_all = shards
        width = key_all.shape[0]
        step_len = width

        def inner(index, state):
            begin = index * step_len
            return attend_part(state, key_all, value_all, offset + begin)

        return lax.fori_loop(0, width // step_len, inner, running)

    start_top = jnp.full((kv_local, group, row_count), NEG_FILL, jnp.float32)
    start_total = jnp.zeros((kv_local, group, row_count), jnp.float32)
    start_accum = jnp.zeros((kv_local, group, row_count, HEAD_DIM), jnp.float32)
    initial = (start_top, start_total, start_accum)
    final_state = absorb(initial, (keys, values), my_start)
    for distance in range(1, DOC_SHARDS + 1):
        earlier = passed_along((keys, values), "seq", distance)
        final_state = absorb(final_state, earlier, my_start - distance * row_count)
    top_last, total_last, accum_last = final_state
    attended = accum_last / total_last[..., None]
    attended = (
        jnp.transpose(attended, (2, 0, 1, 3))
        .reshape(row_count, kv_local * group * HEAD_DIM)
        .astype(jnp.bfloat16)
    )
    partial_terms = jnp.dot(
        attended,
        lax.all_gather(out_weight, "seq", axis=1, tiled=True),
        preferred_element_type=jnp.float32,
    )
    projected = lax.psum_scatter(
        partial_terms.astype(jnp.bfloat16), "exp", scatter_dimension=0, tiled=True
    ).astype(jnp.float32)
    hidden_state = residual.astype(jnp.float32) + projected
    variance = jnp.mean(hidden_state * hidden_state, axis=1, keepdims=True)
    normed = (hidden_state * lax.rsqrt(variance + 1e-06) * norm_gain[None, :]).astype(jnp.bfloat16)
    n_seq = lax.axis_size("seq")
    n_exp = lax.axis_size("exp")
    experts = n_seq * n_exp
    token_count = expert_ids.shape[0]
    topk = expert_ids.shape[1]
    width_d = residual.shape[1]
    capacity = max(2, (token_count * topk * 9 + 8 * experts - 1) // (8 * experts))
    route_count = token_count * topk
    flat_ids = expert_ids.reshape(-1)
    onehot = (flat_ids[:, None] == jnp.arange(experts, dtype=jnp.int32)[None, :]).astype(
        jnp.bfloat16
    )
    route_iota = jnp.arange(route_count, dtype=jnp.int32)
    lower = (route_iota[:, None] > route_iota[None, :]).astype(jnp.bfloat16)
    earlier_counts = jnp.dot(lower, onehot, preferred_element_type=jnp.float32)
    position = jnp.sum(earlier_counts * onehot.astype(jnp.float32), axis=1).astype(jnp.int32)
    slot_index = flat_ids * capacity + position
    source_rows = route_iota // topk
    outbound = (
        jnp.zeros((experts * capacity, width_d), jnp.bfloat16)
        .at[slot_index]
        .set(normed[source_rows])
    )
    outbound = outbound.reshape(experts, capacity, width_d)
    arrived = lax.all_to_all(outbound, ("seq", "exp"), split_axis=0, concat_axis=0, tiled=True)
    shape_in = arrived.shape
    arrived_rows = arrived.reshape(-1, shape_in[2])
    gate_part = jnp.dot(arrived_rows, w_gate[0], preferred_element_type=jnp.float32)
    up_part = jnp.dot(arrived_rows, w_up[0], preferred_element_type=jnp.float32)
    inner_act = (jax.nn.silu(gate_part) * up_part).astype(jnp.bfloat16)
    produced = jnp.dot(inner_act, w_down[0], preferred_element_type=jnp.float32).astype(
        jnp.bfloat16
    )
    answered = produced.reshape(shape_in)
    returned = lax.all_to_all(answered, ("seq", "exp"), split_axis=0, concat_axis=0, tiled=True)
    returned = returned.reshape(experts * capacity, width_d)
    picked = returned[slot_index].reshape(token_count, topk, width_d)
    routed = jnp.sum(picked.astype(jnp.float32) * gate_values[:, :, None], axis=1)
    return (hidden_state + routed).astype(jnp.bfloat16)


def solution(mesh):
    in_specs = (
        P("seq", "exp"),
        P("seq", "exp"),
        P("seq", "exp"),
        P(),
        P("exp", "seq"),
        P(("seq", "exp"), None),
        P(),
        P(("seq", "exp"), None),
        P(("seq", "exp"), None),
        P(("seq", "exp"), None, None),
        P(("seq", "exp"), None, None),
        P(("seq", "exp"), None, None),
    )
    out_specs = P(("seq", "exp"), None)
    return jax.shard_map(body, mesh=mesh, in_specs=in_specs, out_specs=out_specs, check_vma=False)
```

profile of v0, /device:TPU:10, one launch (start us, length us, event | category | flops | bytes accessed | tf_op | source)
XLA Modules:
  0.0 753.2 jit_solution(10169768108697691767)
XLA Ops:
  6.5 0.7 all-gather.2.cloned.1.call-update
  7.3 1.9 collective-permute-start
  9.2 3.4 collective-permute-start.2
  12.6 2.9 collective-permute-start.1
  15.6 3.4 collective-permute-start.3
  19.0 3.0 collective-permute-start.4
  22.1 0.7 copy.41
  22.9 0.1 reduce.12
  23.0 0.1 convert_reduce_fusion
  23.1 3.5 collective-permute-start.5
  26.7 5.2 collective-permute-start.6
  32.0 2.8 collective-permute-start.7
  34.8 3.6 compare_and_fusion
  38.5 1.5 copy.42
  43.0 0.1 broadcast_in_dim.156
  43.2 7.9 %conditional.5 = ((f32[1,8,512]{2,1,0:T(8,128)S(1)}, f32[1,8,512]{2,1,0:T(8,128)S(1)}, f32[1,8,512,128]{3,2,1,0:T(8,128)S(1)})) conditional(s32[]{:T(128)} %convert_element_type.123, (f32[1,8,512]{2,1,0:T(8,128)S(1)}, f32[1,8,512]{2,1,0:T(8,128)S(1)}, f32[1,8,512,128]{3,2,1,0:T(8,128)S(1)}) %tuple.52, (pred[512,512]{0,1:T(8,128)(4,1)}, ...), branch_computations={%region_11.12_spmd, %region_12.0_spmd} | conditional | flops 1102065664 | bytes 33292376 | solution.py:81
  43.2 2.6 fusion
  45.8 2.0 fusion.2
  47.9 3.1 bitcast_add_fusion
  51.0 7.9 %conditional.6 = ((f32[1,8,512]{2,1,0:T(8,128)S(1)}, f32[1,8,512]{2,1,0:T(8,128)S(1)}, f32[1,8,512,128]{3,2,1,0:T(8,128)S(1)})) conditional(s32[]{:T(128)} %convert_element_type.122, (f32[1,8,512]{2,1,0:T(8,128)S(1)}, f32[1,8,512]{2,1,0:T(8,128)S(1)}, f32[1,8,512,128]{3,2,1,0:T(8,128)S(1)}) %get-tuple-element.514, (pred[512,512]{0,1:T(8,128)(4,1)}, ...), branch_computations={%region_15.16_spmd, %region_16.19_spmd} | conditional | flops 1102065664 | bytes 33292376 | solution.py:81
  51.1 2.6 fusion.17
  53.7 2.0 fusion.19
  55.7 3.1 bitcast_add_fusion.2
  58.9 0.5 conditional.7
  59.5 10.8 %conditional.9 = (f32[1,8,512]{2,1,0:T(8,128)S(1)}, f32[1,8,512,128]{2,3,1,0:T(8,128)}) conditional(s32[]{:T(128)} %convert_element_type.116, (f32[1,8,512]{2,1,0:T(8,128)S(1)}, f32[1,8,512,128]{3,2,1,0:T(8,128)S(1)}) %tuple.57, (pred[512,512]{0,1:T(8,128)(4,1)S(1)}, bf16[512,1,8,128]{0,3,2,1:T(8,128)(2,1)S(1)}, bf16[512,128]{1,0:T(8,128)(2,1)}, ...), branch_computations={%region_27.28_spmd, %region_28.0_spmd} | conditional | flops 1102069760 | bytes 69435440 | solution.py:81
  59.5 1.8 copy.57
  70.3 1.9 divide_convert_fusion
  72.2 4.4 all-gather.2.cloned.1.call-done
  76.6 9.6 %convolution_convert_fusion.1 = bf16[512,4096]{1,0:T(8,128)(2,1)} fusion(bf16[512,1024]{0,1:T(8,128)(2,1)S(1)} %bitcast.273, bf16[1024,4096]{1,0:T(8,128)(2,1)} %all-gather.2.cloned.1.call-done), kind=kOutput, calls=%fused_computation.112 | convolution fusion | flops 4297064448 | bytes 13631488 | tf_op jit(solution)/shard_map/dot_general | solution.py:109
  86.3 0.6 fusion.102
  87.2 65.8 %reduce-scatter.2.cloned.1.call-done = bf16[128,4096]{1,0:T(8,128)(2,1)} async-done(((bf16[512,4096]{1,0:T(8,128)(2,1)}), bf16[128,4096]{1,0:T(8,128)(2,1)}) %reduce-scatter.2.cloned.1.call-update) | async-done | bytes 1048592 | tf_op jit(solution)/shard_map/reduce_scatter | solution.py:114
  153.0 1.6 multiply_reduce_fusion
  154.7 1.6 multiply_convert_fusion
  156.3 7.7 %gather_fusion = bf16[1024,4096]{1,0:T(8,128)(2,1)} fusion(bf16[128,4096]{1,0:T(8,128)(2,1)S(1)} %multiply_convert_fusion, s32[1024]{0:T(1024)S(1)} %broadcast_clamp_fusion.1), kind=kCustom, calls=%fused_computation | custom fusion | bytes 16781312 | tf_op jit(solution)/shard_map/gather | solution.py:141
  164.1 18.6 %scatter_custom_fusion = bf16[1152,4096]{1,0:T(8,128)(2,1)} fusion(s32[1024]{0:T(1024)S(1)} %bitcast.283, bf16[1024,4096]{1,0:T(8,128)(2,1)} %gather_fusion, bf16[]{:T(256)} %constant.148.clone.1), kind=kCustom, calls=%fused_computation.113 | custom fusion | bytes 9437696 | tf_op jit(solution)/shard_map/scatter | solution.py:141
  182.7 15.1 %reshape.332 = bf16[128,9,4096]{2,1,0:T(8,128)(2,1)} reshape(bf16[1152,4096]{1,0:T(8,128)(2,1)} %scatter_custom_fusion) | data formatting | bytes 18874368 | tf_op jit(solution)/shard_map/reshape | solution.py:143
  197.8 194.1 %all_to_all.10 = bf16[128,9,4096]{2,1,0:T(8,128)(2,1)} all-to-all(bf16[128,9,4096]{2,1,0:T(8,128)(2,1)} %reshape.332), channel_id=1, replica_groups=mesh['seq'=32,'exp'=4] {'seq','exp'}, dimensions={0} | all-to-all | bytes 18874368 | tf_op jit(solution)/shard_map/all_to_all | solution.py:144
  392.0 15.8 %reshape.333 = bf16[1152,4096]{1,0:T(8,128)(2,1)} reshape(bf16[128,9,4096]{2,1,0:T(8,128)(2,1)} %all_to_all.10) | data formatting | bytes 18874368 | tf_op jit(solution)/shard_map/reshape | solution.py:146
  407.8 12.0 %fusion.90 = f32[1152,768]{1,0:T(8,128)S(1)} fusion(bf16[1152,4096]{1,0:T(8,128)(2,1)} %reshape.333, bf16[1,4096,768]{2,1,0:T(8,128)(2,1)} %param.31), kind=kOutput, calls=%fused_computation.110 | convolution fusion | flops 7247757312 | bytes 19267584 | tf_op jit(solution)/shard_map/dot_general | solution.py:147
  419.9 10.3 %fusion.98 = bf16[1152,768]{1,0:T(8,128)(2,1)S(1)} fusion(bf16[1152,4096]{1,0:T(8,128)(2,1)S(1)} %copy-done.1, bf16[1,4096,768]{2,1,0:T(8,128)(2,1)} %param.32, f32[1152,768]{1,0:T(8,128)S(1)} %fusion.90), kind=kOutput, calls=%fused_computation.118 | convolution fusion | flops 7253065728 | bytes 21037056 | tf_op jit(solution)/shard_map/dot_general | solution.py:148
  430.2 9.6 %convolution_convert_fusion = bf16[1152,4096]{1,0:T(8,128)(2,1)} fusion(bf16[1152,768]{1,0:T(8,128)(2,1)S(1)} %fusion.98, bf16[1,768,4096]{2,1,0:T(8,128)(2,1)S(1)} %bitcast.289), kind=kOutput, calls=%fused_computation.106 | convolution fusion | flops 7252475904 | bytes 17498112 | tf_op jit(solution)/shard_map/dot_general | solution.py:150
  439.7 15.1 %reshape.334 = bf16[128,9,4096]{2,1,0:T(8,128)(2,1)} reshape(bf16[1152,4096]{1,0:T(8,128)(2,1)} %convolution_convert_fusion) | data formatting | bytes 18874368 | tf_op jit(solution)/shard_map/reshape | solution.py:153
  454.8 10.0 %all-to-all-start.1 = ((bf16[128,9,4096]{2,1,0:T(8,128)(2,1)}), bf16[128,9,4096]{2,1,0:T(8,128)(2,1)}, u32[]{:S(2)}, u32[]{:S(2)}) async-start(bf16[128,9,4096]{2,1,0:T(8,128)(2,1)} %reshape.334), calls=%async_computation.2 | async-start | bytes 33554432 | tf_op jit(solution)/shard_map/all_to_all | solution.py:154
  465.0 229.0 %all-to-all-done.1 = bf16[128,9,4096]{2,1,0:T(8,128)(2,1)} async-done(((bf16[128,9,4096]{2,1,0:T(8,128)(2,1)}), bf16[128,9,4096]{2,1,0:T(8,128)(2,1)}, u32[]{:S(2)}, u32[]{:S(2)}) %all-to-all-start.1) | async-done | bytes 9437216 | tf_op jit(solution)/shard_map/all_to_all | solution.py:154
  694.0 15.8 %reshape.335 = bf16[1152,4096]{1,0:T(8,128)(2,1)} reshape(bf16[128,9,4096]{2,1,0:T(8,128)(2,1)} %all-to-all-done.1) | data formatting | bytes 18874368 | tf_op jit(solution)/shard_map/reshape | solution.py:155
  709.9 20.1 %gather_fusion.1 = bf16[1024,4096]{1,0:T(8,128)(2,1)} fusion(bf16[1152,4096]{1,0:T(8,128)(2,1)} %reshape.335, s32[1024]{0:T(1024)S(1)} %broadcast_clamp_fusion), kind=kCustom, calls=%fused_computation.1 | custom fusion | bytes 16781312 | tf_op jit(solution)/shard_map/gather | solution.py:156
  730.0 13.3 %fusion.86 = f32[128,4096]{1,0:T(8,128)} fusion(bf16[1024,4096]{1,0:T(8,128)(2,1)} %gather_fusion.1, f32[128,8]{1,0:T(8,128)S(1)} %copy.51), kind=kLoop, calls=%fused_computation.105 | loop fusion | flops 12058624 | bytes 10489856 | tf_op jit(solution)/shard_map/reduce_sum | solution.py:157
  743.3 2.9 add_convert_fusion
  (70 shorter events, 0.8 us)
Async XLA Ops:
  6.5 70.0 %all-gather.2.cloned.1.call-start = ((), (), s32[]{:S(2)}) async-start(), calls=%async_computation.3 | async-start | bytes 8650752 | tf_op jit(solution)/shard_map/all_gather | solution.py:111
  7.3 145.8 %reduce-scatter.2.cloned.1.call-start = ((), (), s32[]{:S(2)}) async-start(), calls=%async_computation.4 | async-start | bytes 5242880 | tf_op jit(solution)/shard_map/reduce_scatter | solution.py:114
  7.3 15.8 %collective-permute-start = (bf16[512,128]{1,0:T(8,128)(2,1)}, bf16[512,128]{1,0:T(8,128)(2,1)S(1)}, u32[]{:S(2)}, u32[]{:S(2)}) collective-permute-start(bf16[512,128]{1,0:T(8,128)(2,1)} %param.23), channel_id=1, source_target_pairs={{0,4},{4,8},{8,12},{12,16},{16,20},{20,24},{24,28},{28,32},{32,36}... | collective-permute-start | bytes 393224 | tf_op jit(solution)/shard_map/ppermute | solution.py:16
  9.2 22.7 %collective-permute-start.2 = (bf16[512,128]{1,0:T(8,128)(2,1)}, bf16[512,128]{1,0:T(8,128)(2,1)S(1)}, u32[]{:S(2)}, u32[]{:S(2)}) collective-permute-start(bf16[512,128]{1,0:T(8,128)(2,1)} %param.23), channel_id=1, source_target_pairs={{0,8},{4,12},{8,16},{12,20},{16,24},{20,28},{24,32},{28,36},{32,40... | collective-permute-start | bytes 393224 | tf_op jit(solution)/shard_map/ppermute | solution.py:16
  12.6 14.0 %collective-permute-start.1 = (bf16[512,128]{1,0:T(8,128)(2,1)}, bf16[512,128]{1,0:T(8,128)(2,1)S(1)}, u32[]{:S(2)}, u32[]{:S(2)}) collective-permute-start(bf16[512,128]{1,0:T(8,128)(2,1)} %param.24), channel_id=1, source_target_pairs={{0,4},{4,8},{8,12},{12,16},{16,20},{20,24},{24,28},{28,32},{32,36}... | collective-permute-start | bytes 393224 | tf_op jit(solution)/shard_map/ppermute | solution.py:16
  15.6 43.3 %collective-permute-start.3 = (bf16[512,128]{1,0:T(8,128)(2,1)}, bf16[512,128]{1,0:T(8,128)(2,1)}, u32[]{:S(2)}, u32[]{:S(2)}) collective-permute-start(bf16[512,128]{1,0:T(8,128)(2,1)} %param.24), channel_id=1, source_target_pairs={{0,8},{4,12},{8,16},{12,20},{16,24},{20,28},{24,32},{28,36},{32,40... | collective-permute-start | bytes 393224 | tf_op jit(solution)/shard_map/ppermute | solution.py:16
  19.0 40.4 %collective-permute-start.4 = (bf16[512,128]{1,0:T(8,128)(2,1)}, bf16[512,128]{1,0:T(8,128)(2,1)}, u32[]{:S(2)}, u32[]{:S(2)}) collective-permute-start(bf16[512,128]{1,0:T(8,128)(2,1)} %param.23), channel_id=1, source_target_pairs={{0,12},{4,16},{8,20},{12,24},{16,28},{20,32},{24,36},{28,40},{32,4... | collective-permute-start | bytes 393224 | tf_op jit(solution)/shard_map/ppermute | solution.py:16
  23.1 11.7 %copy-start.9 = (bf16[512,128]{1,0:T(8,128)(2,1)}, bf16[512,128]{1,0:T(8,128)(2,1)S(1)}, u32[]{:S(2)}) copy-start(bf16[512,128]{1,0:T(8,128)(2,1)S(1)} %collective-permute-done) | copy-start | bytes 393220
  23.1 36.3 %collective-permute-start.5 = (bf16[512,128]{1,0:T(8,128)(2,1)}, bf16[512,128]{1,0:T(8,128)(2,1)}, u32[]{:S(2)}, u32[]{:S(2)}) collective-permute-start(bf16[512,128]{1,0:T(8,128)(2,1)} %param.24), channel_id=1, source_target_pairs={{0,12},{4,16},{8,20},{12,24},{16,28},{20,32},{24,36},{28,40},{32,4... | collective-permute-start | bytes 393224 | tf_op jit(solution)/shard_map/ppermute | solution.py:16
  26.7 8.1 %copy-start.14 = (bf16[512,128]{1,0:T(8,128)(2,1)}, bf16[512,128]{1,0:T(8,128)(2,1)S(1)}, u32[]{:S(2)}) copy-start(bf16[512,128]{1,0:T(8,128)(2,1)S(1)} %collective-permute-done.1) | copy-start | bytes 393220
  26.7 32.7 %collective-permute-start.6 = (bf16[512,128]{1,0:T(8,128)(2,1)}, bf16[512,128]{1,0:T(8,128)(2,1)}, u32[]{:S(2)}, u32[]{:S(2)}) collective-permute-start(bf16[512,128]{1,0:T(8,128)(2,1)} %param.23), channel_id=1, source_target_pairs={{0,16},{4,20},{8,24},{12,28},{16,32},{20,36},{24,40},{28,44},{32,4... | collective-permute-start | bytes 393224 | tf_op jit(solution)/shard_map/ppermute | solution.py:16
  32.0 2.9 copy-start.8
  32.0 27.5 %collective-permute-start.7 = (bf16[512,128]{1,0:T(8,128)(2,1)}, bf16[512,128]{1,0:T(8,128)(2,1)}, u32[]{:S(2)}, u32[]{:S(2)}) collective-permute-start(bf16[512,128]{1,0:T(8,128)(2,1)} %param.24), channel_id=1, source_target_pairs={{0,16},{4,20},{8,24},{12,28},{16,32},{20,36},{24,40},{28,44},{32,4... | collective-permute-start | bytes 393224 | tf_op jit(solution)/shard_map/ppermute | solution.py:16
  43.2 2.6 copy-start.7
  43.2 4.7 copy-start.13
  51.0 2.6 copy-start.6
  51.0 4.7 copy-start.15
  76.6 9.6 %copy-start.11 = (s32[128,8]{0,1:T(8,128)S(1)}, s32[128,8]{0,1:T(8,128)}, u32[]{:S(2)}) copy-start(s32[128,8]{0,1:T(8,128)} %param.29) | copy-start | bytes 12292
  76.6 76.5 %copy-start.2 = (bf16[128,4096]{1,0:T(8,128)(2,1)S(1)}, bf16[128,4096]{1,0:T(8,128)(2,1)}, u32[]{:S(2)}) copy-start(bf16[128,4096]{1,0:T(8,128)(2,1)} %param.27) | copy-start | bytes 3145732
  86.1 68.6 %copy-start.10 = (f32[4096]{0:T(1024)S(1)}, f32[4096]{0:T(1024)}, u32[]{:S(2)}) copy-start(f32[4096]{0:T(1024)} %param.28) | copy-start | bytes 49156
  407.8 12.0 %copy-start.1 = (bf16[1152,4096]{1,0:T(8,128)(2,1)S(1)}, bf16[1152,4096]{1,0:T(8,128)(2,1)}, u32[]{:S(2)}) copy-start(bf16[1152,4096]{1,0:T(8,128)(2,1)} %reshape.333) | copy-start | bytes 28311556
  407.8 22.3 %slice-start = ((s8[6291456]{0:T(1024)(128)(4,1)}), s8[4194304]{0:T(1024)(128)(4,1)S(1)}, s32[]{:S(2)}) async-start(s8[6291456]{0:T(1024)(128)(4,1)} %bitcast.288), calls=%async_computation.5 | async-start | bytes 8388608
  419.8 10.3 %slice-start.1 = ((s8[6291456]{0:T(1024)(128)(4,1)}), s8[2097152]{0:T(1024)(128)(4,1)S(1)}, s32[]{:S(2)}) async-start(s8[6291456]{0:T(1024)(128)(4,1)} %bitcast.288), calls=%async_computation.6 | async-start | bytes 4194304
  454.8 10.0 %copy-start.12 = (f32[128,8]{0,1:T(8,128)S(1)}, f32[128,8]{0,1:T(8,128)}, u32[]{:S(2)}) copy-start(f32[128,8]{0,1:T(8,128)} %param.30) | copy-start | bytes 12292
  454.8 239.2 %all-to-all-start.1 = ((bf16[128,9,4096]{2,1,0:T(8,128)(2,1)}), bf16[128,9,4096]{2,1,0:T(8,128)(2,1)}, u32[]{:S(2)}, u32[]{:S(2)}) async-start(bf16[128,9,4096]{2,1,0:T(8,128)(2,1)} %reshape.334), calls=%async_computation.2 | async-start | bytes 33554432 | tf_op jit(solution)/shard_map/all_to_all | solution.py:154
  730.0 13.3 %copy-start.3 = (bf16[128,4096]{1,0:T(8,128)(2,1)S(1)}, bf16[128,4096]{1,0:T(8,128)(2,1)}, u32[]{:S(2)}) copy-start(bf16[128,4096]{1,0:T(8,128)(2,1)} %reduce-scatter.2.cloned.1.call-done) | copy-start | bytes 3145732
Sparse Core Ops, SparseCore 0:
  9.5 66.9 all-gather.1
  86.3 66.7 reduce-scatter.1
where the time goes:
time: 762 us; the launch traced here: 753 us
  waiting for transfers between devices  300 us (39%)
  blocking collectives  194 us (25%)
  local copies, waits for them, and re-layouts  113 us (15%)
  matrix products  53.4 us (7%)
  starting transfers between devices  36.4 us (5%)
  other arithmetic  29.4 us (4%)
  between operations  17.1 us (2%)
  loops' own time  9.67 us (1%)
    all_to_all x1, waiting for transfers between devices, body(): lax.all_to_all(answered, ('seq', 'exp'), split_axis=0, concat_axis=0, til...  229 us
    all_to_all x1, blocking collectives, body(): lax.all_to_all(outbound, ('seq', 'exp'), split_axis=0, concat_axis=0, til...  194 us
    reduce_scatter x1, waiting for transfers between devices, body(): lax.psum_scatter(partial_terms.astype(jnp.bfloat16), 'exp', scatter_dimen...  65.8 us
    ppermute x8, starting transfers between devices, passed_along(): return lax.ppermute(x, axis, pairs)  26.3 us
    gather x1, local copies, waits for them, and re-layouts, body(): picked = returned[slot_index].reshape(token_count, topk, width_d)  20.1 us
    scatter x1, local copies, waits for them, and re-layouts, body(): outbound = jnp.zeros((experts * capacity, width_d), jnp.bfloat16).at[slot...  18.6 us
    reshape x1, local copies, waits for them, and re-layouts, body(): arrived_rows = arrived.reshape(-1, shape_in[2])  15.8 us
    reshape x1, local copies, waits for them, and re-layouts, body(): returned = returned.reshape(experts * capacity, width_d)  15.8 us
  transfers between devices with their start and end apart: 11, of which 3 were waited for; matrix products, arithmetic and copies ran while one was open for 4% of the time, Pallas kernels for 0%

commit v1 on v0

--- a/solution.py
+++ b/solution.py
@@ -1,13 +1,260 @@
+import functools
+
 import jax
 import jax.numpy as jnp
 from jax import lax
+from jax.experimental import pallas as pl
+from jax.experimental.pallas import tpu as pltpu
 from jax.sharding import PartitionSpec as P
 
 HEAD_DIM = 128
 DOC_SHARDS = 4
-
-
 NEG_FILL = -1e30
+D = 4096
+HALF = D // 2
+FFH = 768
+CAP = 9
+DEVICES = 128
+GROUPS = 4
+PER_GROUP = DEVICES // GROUPS
+MAIN = PER_GROUP * 8
+ROWS = PER_GROUP * CAP
+EXTRA = D // 16
+MESSAGE = HALF + EXTRA
+CHUNK = 512
+STRIDE = 37
+MESH = pl.DeviceIdType.MESH
+
+
+def place():
+    seq = lax.axis_index("seq")
+    return seq // 8, (seq // 2) % 4, seq % 2, lax.axis_index("exp")
+
+
+def route_target(index):
+    y, x, c, z = place()
+    j = (index * STRIDE) % DEVICES
+    dy, dx, dc, dz = j // 32, (j // 8) % 4, (j // 4) % 2, j % 4
+    ey = jnp.where(c == 0, dy, dx)
+    ex = jnp.where(c == 0, dx, dz)
+    ez = jnp.where(c == 0, dz, dy)
+    return (y + ey) % 4, (x + ex) % 4, (c + dc) % 2, (z + ez) % 4
+
+
+def route_source(index):
+    y, x, c, z = place()
+    j = (index * STRIDE) % DEVICES
+    dy, dx, dc, dz = j // 32, (j // 8) % 4, (j // 4) % 2, j % 4
+    sc = (c + dc) % 2
+    ey = jnp.where(sc == 0, dy, dx)
+    ex = jnp.where(sc == 0, dx, dz)
+    ez = jnp.where(sc == 0, dz, dy)
+    return (y - ey + 4) % 4, (x - ex + 4) % 4, sc, (z - ez + 4) % 4
+
+
+def device(y, x, c, z):
+    return {"seq": (y * 4 + x) * 2 + c, "exp": z}
+
+
+def moe_kernel(
+    normed, hidden, picks, gates, perm, perm_t, w_gate, w_up, w_down, out,
+    outbound, arrived, returned, wg, wu, wd, rows, extra, acc,
+    weight_sem, send_sem, recv_sem, back_send_sem, back_recv_sem,
+):
+    loads = [
+        pltpu.make_async_copy(src.at[0], dst, weight_sem.at[k])
+        for k, (src, dst) in enumerate(((w_gate, wg), (w_up, wu), (w_down, wd)))
+    ]
+    for load in loads:
+        load.start()
+
+    def pack(buffer, first, c, left, right):
+        both = jnp.concatenate(
+            [left.reshape(PER_GROUP, 8, CHUNK), right.reshape(PER_GROUP, 8, CHUNK)], axis=1
+        )
+        buffer[pl.ds(first, PER_GROUP), :, c : c + CHUNK] = both.astype(jnp.bfloat16)
+
+    def pack_extra(buffer, first):
+        stacked = jnp.concatenate(
+            [extra[:, j * EXTRA : (j + 1) * EXTRA] for j in range(16)], axis=0
+        ).astype(jnp.bfloat16)
+        turned = jnp.dot(perm_t[...], stacked, preferred_element_type=jnp.float32)
+        buffer[pl.ds(first, PER_GROUP), :, HALF:MESSAGE] = turned.astype(jnp.bfloat16).reshape(
+            PER_GROUP, 16, EXTRA
+        )
+
+    def unpack(buffer, first):
+        for c in range(0, HALF, CHUNK):
+            both = buffer[pl.ds(first, PER_GROUP), :, c : c + CHUNK].astype(jnp.float32)
+            rows[0:MAIN, c : c + CHUNK] = both[:, 0:8].reshape(MAIN, CHUNK).astype(jnp.bfloat16)
+            rows[0:MAIN, HALF + c : HALF + c + CHUNK] = (
+                both[:, 8:16].reshape(MAIN, CHUNK).astype(jnp.bfloat16)
+            )
+        stacked = buffer[pl.ds(first, PER_GROUP), :, HALF:MESSAGE].reshape(PER_GROUP * 16, EXTRA)
+        turned = jnp.dot(perm[...], stacked, preferred_element_type=jnp.float32)
+        for j in range(16):
+            rows[MAIN:ROWS, j * EXTRA : (j + 1) * EXTRA] = turned[
+                j * PER_GROUP : (j + 1) * PER_GROUP
+            ].astype(jnp.bfloat16)
+
+    def build(g, carry):
+        first = g * PER_GROUP
+        for c in range(0, HALF, CHUNK):
+            halves = []
+            for base in (c, HALF + c):
+                got = jnp.dot(
+                    picks[g], normed[:, base : base + CHUNK], preferred_element_type=jnp.float32
+                )
+                extra[:, base : base + CHUNK] = got[MAIN:ROWS]
+                halves.append(got[0:MAIN])
+            pack(outbound, first, c, *halves)
+        pack_extra(outbound, first)
+
+        def send(k, carry):
+            index = first + k
+
+            @pl.when(index == 0)
+            def _():
+                pltpu.make_async_copy(outbound.at[0], arrived.at[0], recv_sem.at[0]).start()
+
+            @pl.when(index > 0)
+            def _():
+                pltpu.make_async_remote_copy(
+                    src_ref=outbound.at[index],
+                    dst_ref=arrived.at[index],
+                    send_sem=send_sem,
+                    recv_sem=recv_sem.at[g],
+                    device_id=device(*route_target(index)),
+                    device_id_type=MESH,
+                ).start()
+
+            return carry
+
+        return lax.fori_loop(0, PER_GROUP, send, carry)
+
+    lax.fori_loop(0, GROUPS, build, 0)
+    for load in loads:
+        load.wait()
+
+    def expert(g, carry):
+        first = g * PER_GROUP
+        block = arrived.at[pl.ds(first, PER_GROUP)]
+        pltpu.make_async_copy(block, block, recv_sem.at[g]).wait()
+        unpack(arrived, first)
+        gate_part = jnp.dot(rows[...], wg[...], preferred_element_type=jnp.float32)
+        up_part = jnp.dot(rows[...], wu[...], preferred_element_type=jnp.float32)
+        inner = (gate_part / (1.0 + jnp.exp(-gate_part)) * up_part).astype(jnp.bfloat16)
+        for c in range(0, HALF, CHUNK):
+            halves = []
+            for base in (c, HALF + c):
+                got = jnp.dot(
+                    inner, wd[:, base : base + CHUNK], preferred_element_type=jnp.float32
+                )
+                extra[:, base : base + CHUNK] = got[MAIN:ROWS]
+                halves.append(got[0:MAIN])
+            pack(arrived, first, c, *halves)
+        pack_extra(arrived, first)
+
+        def send(k, carry):
+            index = first + k
+
+            @pl.when(index == 0)
+            def _():
+                pltpu.make_async_copy(arrived.at[0], returned.at[0], back_recv_sem.at[0]).start()
+
+            @pl.when(index > 0)
+            def _():
+                pltpu.make_async_remote_copy(
+                    src_ref=arrived.at[index],
+                    dst_ref=returned.at[index],
+                    send_sem=back_send_sem,
+                    recv_sem=back_recv_sem.at[g],
+                    device_id=device(*route_source(index)),
+                    device_id_type=MESH,
+                ).start()
+
+            return carry
+
+        return lax.fori_loop(0, PER_GROUP, send, carry)
+
+    lax.fori_loop(0, GROUPS, expert, 0)
+    acc[...] = hidden[...]
+
+    def combine(g, carry):
+        first = g * PER_GROUP
+        block = returned.at[pl.ds(first, PER_GROUP)]
+        pltpu.make_async_copy(block, block, back_recv_sem.at[g]).wait()
+        unpack(returned, first)
+        gate = gates[g]
+        high = gate.astype(jnp.bfloat16)
+        low = (gate - high.astype(jnp.float32)).astype(jnp.bfloat16)
+        both = jnp.concatenate([high, low], axis=0)
+        for c in range(0, D, CHUNK):
+            got = jnp.dot(both, rows[:, c : c + CHUNK], preferred_element_type=jnp.float32)
+            acc[:, c : c + CHUNK] += got[0:128] + got[128:256]
+        return carry
+
+    lax.fori_loop(0, GROUPS, combine, 0)
+    out[...] = acc[...].astype(jnp.bfloat16)
+    sent = outbound.at[pl.ds(1, DEVICES - 1)]
+    pltpu.make_async_copy(sent, sent, send_sem).wait()
+    sent = arrived.at[pl.ds(1, DEVICES - 1)]
+    pltpu.make_async_copy(sent, sent, back_send_sem).wait()
+
+
+def routed_layer(normed, hidden, expert_ids, gate_values, w_gate, w_up, w_down):
+    tokens = normed.shape[0]
+    ty, tx, tc, tz = route_target(jnp.arange(DEVICES, dtype=jnp.int32))
+    target = ((ty * 4 + tx) * 2 + tc) * 4 + tz
+    hit = (expert_ids.T[None, :, :] == target[:, None, None])
+    member = jnp.any(hit, axis=1)
+    gate = jnp.sum(jnp.where(hit, gate_values.T[None, :, :], 0.0), axis=1)
+    before = jnp.triu(jnp.ones((tokens, tokens), jnp.bfloat16), 1)
+    position = jnp.dot(member.astype(jnp.bfloat16), before, preferred_element_type=jnp.float32)
+    position = jnp.where(member, position, -1.0)
+    slot = position[:, None, :] == jnp.arange(CAP, dtype=jnp.float32)[None, :, None]
+
+    def grouped(x):
+        x = x.reshape(GROUPS, PER_GROUP, CAP, tokens)
+        main = x[:, :, :8].reshape(GROUPS, MAIN, tokens)
+        return jnp.concatenate([main, x[:, :, 8]], axis=1)
+
+    picks = grouped(slot.astype(jnp.bfloat16))
+    gates = jnp.swapaxes(grouped(jnp.where(slot, gate[:, None, :], 0.0)), 1, 2)
+    line = jnp.arange(16 * PER_GROUP, dtype=jnp.int32)
+    origin = (line % PER_GROUP) * 16 + line // PER_GROUP
+    perm = (origin[:, None] == line[None, :]).astype(jnp.bfloat16)
+    perm_t = (line[:, None] == origin[None, :]).astype(jnp.bfloat16)
+    vmem = pl.BlockSpec(memory_space=pltpu.VMEM)
+    anywhere = pl.BlockSpec(memory_space=pl.ANY)
+    return pl.pallas_call(
+        moe_kernel,
+        out_shape=jax.ShapeDtypeStruct((tokens, D), jnp.bfloat16),
+        in_specs=[vmem] * 6 + [anywhere] * 3,
+        out_specs=vmem,
+        scratch_shapes=[
+            pltpu.VMEM((DEVICES, 16, MESSAGE), jnp.bfloat16),
+            pltpu.VMEM((DEVICES, 16, MESSAGE), jnp.bfloat16),
+            pltpu.VMEM((DEVICES, 16, MESSAGE), jnp.bfloat16),
+            pltpu.VMEM((D, FFH), jnp.bfloat16),
+            pltpu.VMEM((D, FFH), jnp.bfloat16),
+            pltpu.VMEM((FFH, D), jnp.bfloat16),
+            pltpu.VMEM((ROWS, D), jnp.bfloat16),
+            pltpu.VMEM((PER_GROUP, D), jnp.float32),
+            pltpu.VMEM((tokens, D), jnp.float32),
+            pltpu.SemaphoreType.DMA((3,)),
+            pltpu.SemaphoreType.DMA,
+            pltpu.SemaphoreType.DMA((GROUPS,)),
+            pltpu.SemaphoreType.DMA,
+            pltpu.SemaphoreType.DMA((GROUPS,)),
+        ],
+        compiler_params=pltpu.CompilerParams(
+            has_side_effects=True, vmem_limit_bytes=63 * 1024 * 1024
+        ),
+        cost_estimate=pl.CostEstimate(
+            flops=24 * 10**9, bytes_accessed=40 * 10**6, transcendentals=10**6
+        ),
+    )(normed, hidden, picks, gates, perm, perm_t, w_gate, w_up, w_down)
 
 
 def passed_along(x, axis, by):
@@ -117,45 +364,7 @@
     hidden_state = residual.astype(jnp.float32) + projected
     variance = jnp.mean(hidden_state * hidden_state, axis=1, keepdims=True)
     normed = (hidden_state * lax.rsqrt(variance + 1e-06) * norm_gain[None, :]).astype(jnp.bfloat16)
-    n_seq = lax.axis_size("seq")
-    n_exp = lax.axis_size("exp")
-    experts = n_seq * n_exp
-    token_count = expert_ids.shape[0]
-    topk = expert_ids.shape[1]
-    width_d = residual.shape[1]
-    capacity = max(2, (token_count * topk * 9 + 8 * experts - 1) // (8 * experts))
-    route_count = token_count * topk
-    flat_ids = expert_ids.reshape(-1)
-    onehot = (flat_ids[:, None] == jnp.arange(experts, dtype=jnp.int32)[None, :]).astype(
-        jnp.bfloat16
-    )
-    route_iota = jnp.arange(route_count, dtype=jnp.int32)
-    lower = (route_iota[:, None] > route_iota[None, :]).astype(jnp.bfloat16)
-    earlier_counts = jnp.dot(lower, onehot, preferred_element_type=jnp.float32)
-    position = jnp.sum(earlier_counts * onehot.astype(jnp.float32), axis=1).astype(jnp.int32)
-    slot_index = flat_ids * capacity + position
-    source_rows = route_iota // topk
-    outbound = (
-        jnp.zeros((experts * capacity, width_d), jnp.bfloat16)
-        .at[slot_index]
-        .set(normed[source_rows])
-    )
-    outbound = outbound.reshape(experts, capacity, width_d)
-    arrived = lax.all_to_all(outbound, ("seq", "exp"), split_axis=0, concat_axis=0, tiled=True)
-    shape_in = arrived.shape
-    arrived_rows = arrived.reshape(-1, shape_in[2])
-    gate_part = jnp.dot(arrived_rows, w_gate[0], preferred_element_type=jnp.float32)
-    up_part = jnp.dot(arrived_rows, w_up[0], preferred_element_type=jnp.float32)
-    inner_act = (jax.nn.silu(gate_part) * up_part).astype(jnp.bfloat16)
-    produced = jnp.dot(inner_act, w_down[0], preferred_element_type=jnp.float32).astype(
-        jnp.bfloat16
-    )
-    answered = produced.reshape(shape_in)
-    returned = lax.all_to_all(answered, ("seq", "exp"), split_axis=0, concat_axis=0, tiled=True)
-    returned = returned.reshape(experts * capacity, width_d)
-    picked = returned[slot_index].reshape(token_count, topk, width_d)
-    routed = jnp.sum(picked.astype(jnp.float32) * gate_values[:, :, None], axis=1)
-    return (hidden_state + routed).astype(jnp.bfloat16)
+    return routed_layer(normed, hidden_state, expert_ids, gate_values, w_gate, w_up, w_down)
 
 
 def solution(mesh):

time: 762 us -> 409 us (0.54)
  the two profiles are of different devices: /device:TPU:10 before, /device:TPU:1 now
where the time goes in v1:
time: 409 us; the launch traced here: 401 us
  Pallas kernels  238 us (58%)
  waiting for transfers between devices  51.2 us (13%)
  starting transfers between devices  29.3 us (7%)
  other arithmetic  22.6 us (6%)
  matrix products  21 us (5%)
  between operations  17 us (4%)
  local copies, waits for them, and re-layouts  15.6 us (4%)
  loops' own time  6.34 us (2%)
    pallas_call x1, Pallas kernels, routed_layer(): pl.pallas_call(moe_kernel, out_shape=jax.ShapeDtypeStruct((tokens, D), jn...  238 us
    reduce_scatter x1, waiting for transfers between devices, body(): lax.psum_scatter(partial_terms.astype(jnp.bfloat16), 'exp', scatter_dimen...  42.9 us
    ppermute x8, starting transfers between devices, passed_along(): return lax.ppermute(x, axis, pairs)  29.3 us
    dot_general x1, matrix products, body(): jnp.dot(attended, lax.all_gather(out_weight, 'seq', axis=1, tiled=True),...  9.48 us
  transfers between devices with their start and end apart: 10, of which 2 were waited for; matrix products, arithmetic and copies ran while one was open for 10% of the time, Pallas kernels for 0%

profile of v1, /device:TPU:1, one launch (start us, length us, event | category | flops | bytes accessed | tf_op | source)
XLA Modules:
  0.0 401.2 jit_solution(5100954343190004335)
XLA Ops:
  6.5 0.7 all-gather.2.cloned.1.call-update
  7.3 4.5 %collective-permute-start = (bf16[512,128]{1,0:T(8,128)(2,1)}, bf16[512,128]{1,0:T(8,128)(2,1)S(1)}, u32[]{:S(2)}, u32[]{:S(2)}) collective-permute-start(bf16[512,128]{1,0:T(8,128)(2,1)} %param.23), channel_id=1, source_target_pairs={{0,4},{4,8},{8,12},{12,16},{16,20},{20,24},{24,28},{28,32},{32,36}... | collective-permute-start | bytes 393224 | tf_op jit(solution)/shard_map/ppermute | solution.py:263
  11.8 3.1 collective-permute-start.2
  15.0 2.2 collective-permute-start.1
  17.2 3.5 collective-permute-start.3
  20.6 5.0 %collective-permute-start.4 = (bf16[512,128]{1,0:T(8,128)(2,1)}, bf16[512,128]{1,0:T(8,128)(2,1)}, u32[]{:S(2)}, u32[]{:S(2)}) collective-permute-start(bf16[512,128]{1,0:T(8,128)(2,1)} %param.23), channel_id=1, source_target_pairs={{0,12},{4,16},{8,20},{12,24},{16,28},{20,32},{24,36},{28,40},{32,4... | collective-permute-start | bytes 393224 | tf_op jit(solution)/shard_map/ppermute | solution.py:263
  25.8 0.7 copy.45
  26.5 0.1 reduce.12
  26.8 3.1 collective-permute-start.5
  29.9 3.2 collective-permute-start.6
  33.0 4.7 %collective-permute-start.7 = (bf16[512,128]{1,0:T(8,128)(2,1)}, bf16[512,128]{1,0:T(8,128)(2,1)}, u32[]{:S(2)}, u32[]{:S(2)}) collective-permute-start(bf16[512,128]{1,0:T(8,128)(2,1)} %param.24), channel_id=1, source_target_pairs={{0,16},{4,20},{8,24},{12,28},{16,32},{20,36},{24,40},{28,44},{32,4... | collective-permute-start | bytes 393224 | tf_op jit(solution)/shard_map/ppermute | solution.py:263
  37.7 3.5 compare_and_fusion
  44.3 1.5 copy.46
  45.8 0.1 broadcast_in_dim.193
  45.9 7.9 %conditional.5 = ((f32[1,8,512]{2,1,0:T(8,128)S(1)}, f32[1,8,512]{2,1,0:T(8,128)S(1)}, f32[1,8,512,128]{3,2,1,0:T(8,128)S(1)})) conditional(s32[]{:T(128)} %convert_element_type.99, (f32[1,8,512]{2,1,0:T(8,128)S(1)}, f32[1,8,512]{2,1,0:T(8,128)S(1)}, f32[1,8,512,128]{3,2,1,0:T(8,128)S(1)}) %tuple.52, (pred[512,512]{0,1:T(8,128)(4,1)}, ...), branch_computations={%region_11.12_spmd, %region_12.0_spmd} | conditional | flops 1102065664 | bytes 33292376 | solution.py:328
  46.0 2.6 fusion
  48.6 2.0 fusion.2
  50.7 3.1 bitcast_add_fusion
  53.8 7.8 %conditional.6 = ((f32[1,8,512]{2,1,0:T(8,128)S(1)}, f32[1,8,512]{2,1,0:T(8,128)S(1)}, f32[1,8,512,128]{3,2,1,0:T(8,128)S(1)})) conditional(s32[]{:T(128)} %convert_element_type.98, (f32[1,8,512]{2,1,0:T(8,128)S(1)}, f32[1,8,512]{2,1,0:T(8,128)S(1)}, f32[1,8,512,128]{3,2,1,0:T(8,128)S(1)}) %get-tuple-element.518, (pred[512,512]{0,1:T(8,128)(4,1)}, ...), branch_computations={%region_15.16_spmd, %region_16.19_spmd} | conditional | flops 1102065664 | bytes 33292376 | solution.py:328
  53.8 2.6 fusion.17
  56.4 2.0 fusion.19
  58.5 3.1 bitcast_add_fusion.2
  61.7 0.5 conditional.7
  62.2 7.5 %conditional.9 = (f32[1,8,512]{2,1,0:T(8,128)S(1)}, f32[1,8,512,128]{2,3,1,0:T(8,128)}) conditional(s32[]{:T(128)} %convert_element_type.92, (f32[1,8,512]{2,1,0:T(8,128)S(1)}, f32[1,8,512,128]{3,2,1,0:T(8,128)S(1)}) %tuple.57, (pred[512,512]{0,1:T(8,128)(4,1)S(1)}, bf16[512,1,8,128]{0,3,2,1:T(8,128)(2,1)S(1)}, bf16[512,128]{1,0:T(8,128)(2,1)}, ...), branch_computations={%region_27.28_spmd, %region_28.0_spmd} | conditional | flops 1102069760 | bytes 35880976 | solution.py:328
  62.2 1.8 copy.64
  69.7 2.1 divide_convert_fusion
  71.8 7.6 %all-gather.2.cloned.1.call-done = bf16[1024,4096]{1,0:T(8,128)(2,1)} async-done(((bf16[1024,128]{1,0:T(8,128)(2,1)}), bf16[1024,4096]{1,0:T(8,128)(2,1)}) %all-gather.2.cloned.1.call-update) | async-done | bytes 8388624 | tf_op jit(solution)/shard_map/all_gather | solution.py:358
  79.4 9.5 %convolution_convert_fusion = bf16[512,4096]{1,0:T(8,128)(2,1)} fusion(bf16[512,1024]{0,1:T(8,128)(2,1)S(1)} %bitcast.265, bf16[1024,4096]{1,0:T(8,128)(2,1)} %all-gather.2.cloned.1.call-done), kind=kOutput, calls=%fused_computation.101 | convolution fusion | flops 4297064448 | bytes 13631488 | tf_op jit(solution)/shard_map/dot_general | solution.py:356
  89.0 0.3 compare_reduce_fusion
  89.3 0.1 convolution_select_fusion
  89.4 0.1 copy.53
  89.6 0.3 fusion.87
  89.9 0.3 copy-done.5
  90.5 1.1 copy.54
  91.6 0.2 fusion.90
  91.8 0.8 copy.56
  92.7 1.3 fusion.86
  94.0 1.5 slice.18
  95.5 3.0 copy.57
  98.5 2.0 copy.58
  100.5 1.7 pad_maximum_fusion.picks
  102.2 2.0 maximum_bitcast_fusion.gates
  104.2 1.1 fusion.89
  105.3 42.9 %reduce-scatter.2.cloned.1.call-done = bf16[128,4096]{1,0:T(8,128)(2,1)} async-done(((bf16[512,4096]{1,0:T(8,128)(2,1)}), bf16[128,4096]{1,0:T(8,128)(2,1)}) %reduce-scatter.2.cloned.1.call-update) | async-done | bytes 1048592 | tf_op jit(solution)/shard_map/reduce_scatter | solution.py:361
  148.2 2.9 convert_add_fusion
  151.1 2.6 multiply_convert_fusion.normed
  153.7 238.1 %shard_map.118 = bf16[128,4096]{1,0:T(8,128)(2,1)} custom-call(bf16[128,4096]{1,0:T(8,128)(2,1)} %multiply_convert_fusion.normed, f32[128,4096]{1,0:T(8,128)} %get-tuple-element.468.hidden, bf16[4,288,128]{2,1,0:T(8,128)(2,1)} %pad_maximum_fusion.picks, f32[4,128,288]{2,1,0:T(8,128)} %maximum_bitcast_fusion.gates, bf16[512,512]{1,0:T(8,128)(2,1)} %get-tuple-element.481.perm, ...), custom_call_target="tpu_custom_call" | custom-call | flops 24000000000 | bytes 40000000 | tf_op jit(solution)/shard_map/pallas_call | solution.py:230
  391.8 2.3 copy.95
  (58 shorter events, 0.7 us)
Async XLA Ops:
  6.5 72.9 %all-gather.2.cloned.1.call-start = ((), (), s32[]{:S(2)}) async-start(), calls=%async_computation.1 | async-start | bytes 8650752 | tf_op jit(solution)/shard_map/all_gather | solution.py:358
  7.3 140.9 %reduce-scatter.2.cloned.1.call-start = ((), (), s32[]{:S(2)}) async-start(), calls=%async_computation.2 | async-start | bytes 5242880 | tf_op jit(solution)/shard_map/reduce_scatter | solution.py:361
  7.3 19.5 %collective-permute-start = (bf16[512,128]{1,0:T(8,128)(2,1)}, bf16[512,128]{1,0:T(8,128)(2,1)S(1)}, u32[]{:S(2)}, u32[]{:S(2)}) collective-permute-start(bf16[512,128]{1,0:T(8,128)(2,1)} %param.23), channel_id=1, source_target_pairs={{0,4},{4,8},{8,12},{12,16},{16,20},{20,24},{24,28},{28,32},{32,36}... | collective-permute-start | bytes 393224 | tf_op jit(solution)/shard_map/ppermute | solution.py:263
  11.8 21.2 %collective-permute-start.2 = (bf16[512,128]{1,0:T(8,128)(2,1)}, bf16[512,128]{1,0:T(8,128)(2,1)S(1)}, u32[]{:S(2)}, u32[]{:S(2)}) collective-permute-start(bf16[512,128]{1,0:T(8,128)(2,1)} %param.23), channel_id=1, source_target_pairs={{0,8},{4,12},{8,16},{12,20},{16,24},{20,28},{24,32},{28,36},{32,40... | collective-permute-start | bytes 393224 | tf_op jit(solution)/shard_map/ppermute | solution.py:263
  15.0 14.9 %collective-permute-start.1 = (bf16[512,128]{1,0:T(8,128)(2,1)}, bf16[512,128]{1,0:T(8,128)(2,1)S(1)}, u32[]{:S(2)}, u32[]{:S(2)}) collective-permute-start(bf16[512,128]{1,0:T(8,128)(2,1)} %param.24), channel_id=1, source_target_pairs={{0,4},{4,8},{8,12},{12,16},{16,20},{20,24},{24,28},{28,32},{32,36}... | collective-permute-start | bytes 393224 | tf_op jit(solution)/shard_map/ppermute | solution.py:263
  17.2 44.5 %collective-permute-start.3 = (bf16[512,128]{1,0:T(8,128)(2,1)}, bf16[512,128]{1,0:T(8,128)(2,1)}, u32[]{:S(2)}, u32[]{:S(2)}) collective-permute-start(bf16[512,128]{1,0:T(8,128)(2,1)} %param.24), channel_id=1, source_target_pairs={{0,8},{4,12},{8,16},{12,20},{16,24},{20,28},{24,32},{28,36},{32,40... | collective-permute-start | bytes 393224 | tf_op jit(solution)/shard_map/ppermute | solution.py:263
  20.6 41.5 %collective-permute-start.4 = (bf16[512,128]{1,0:T(8,128)(2,1)}, bf16[512,128]{1,0:T(8,128)(2,1)}, u32[]{:S(2)}, u32[]{:S(2)}) collective-permute-start(bf16[512,128]{1,0:T(8,128)(2,1)} %param.23), channel_id=1, source_target_pairs={{0,12},{4,16},{8,20},{12,24},{16,28},{20,32},{24,36},{28,40},{32,4... | collective-permute-start | bytes 393224 | tf_op jit(solution)/shard_map/ppermute | solution.py:263
  26.8 10.9 %copy-start.7 = (bf16[512,128]{1,0:T(8,128)(2,1)}, bf16[512,128]{1,0:T(8,128)(2,1)S(1)}, u32[]{:S(2)}) copy-start(bf16[512,128]{1,0:T(8,128)(2,1)S(1)} %collective-permute-done) | copy-start | bytes 393220
  26.8 35.4 %collective-permute-start.5 = (bf16[512,128]{1,0:T(8,128)(2,1)}, bf16[512,128]{1,0:T(8,128)(2,1)}, u32[]{:S(2)}, u32[]{:S(2)}) collective-permute-start(bf16[512,128]{1,0:T(8,128)(2,1)} %param.24), channel_id=1, source_target_pairs={{0,12},{4,16},{8,20},{12,24},{16,28},{20,32},{24,36},{28,40},{32,4... | collective-permute-start | bytes 393224 | tf_op jit(solution)/shard_map/ppermute | solution.py:263
  29.9 15.9 %copy-start.12 = (bf16[512,128]{1,0:T(8,128)(2,1)}, bf16[512,128]{1,0:T(8,128)(2,1)S(1)}, u32[]{:S(2)}) copy-start(bf16[512,128]{1,0:T(8,128)(2,1)S(1)} %collective-permute-done.1) | copy-start | bytes 393220
  29.9 32.3 %collective-permute-start.6 = (bf16[512,128]{1,0:T(8,128)(2,1)}, bf16[512,128]{1,0:T(8,128)(2,1)}, u32[]{:S(2)}, u32[]{:S(2)}) collective-permute-start(bf16[512,128]{1,0:T(8,128)(2,1)} %param.23), channel_id=1, source_target_pairs={{0,16},{4,20},{8,24},{12,28},{16,32},{20,36},{24,40},{28,44},{32,4... | collective-permute-start | bytes 393224 | tf_op jit(solution)/shard_map/ppermute | solution.py:263
  33.0 4.7 %copy-start.6 = (bf16[512,128]{1,0:T(8,128)(2,1)}, bf16[512,128]{1,0:T(8,128)(2,1)S(1)}, u32[]{:S(2)}) copy-start(bf16[512,128]{1,0:T(8,128)(2,1)S(1)} %collective-permute-done.2) | copy-start | bytes 393220
  33.0 29.2 %collective-permute-start.7 = (bf16[512,128]{1,0:T(8,128)(2,1)}, bf16[512,128]{1,0:T(8,128)(2,1)}, u32[]{:S(2)}, u32[]{:S(2)}) collective-permute-start(bf16[512,128]{1,0:T(8,128)(2,1)} %param.24), channel_id=1, source_target_pairs={{0,16},{4,20},{8,24},{12,28},{16,32},{20,36},{24,40},{28,44},{32,4... | collective-permute-start | bytes 393224 | tf_op jit(solution)/shard_map/ppermute | solution.py:263
  46.0 2.6 copy-start.4
  46.0 4.7 %copy-start.11 = (bf16[512,128]{1,0:T(8,128)(2,1)S(1)}, bf16[512,128]{1,0:T(8,128)(2,1)}, u32[]{:S(2)}) copy-start(bf16[512,128]{1,0:T(8,128)(2,1)} %get-tuple-element.257) | copy-start | bytes 393220 | tf_op jit(solution)/shard_map/while/body/eval_jaxpr/cond
  53.8 2.6 copy-start.3
  53.8 4.7 %copy-start.13 = (bf16[512,128]{1,0:T(8,128)(2,1)S(1)}, bf16[512,128]{1,0:T(8,128)(2,1)}, u32[]{:S(2)}) copy-start(bf16[512,128]{1,0:T(8,128)(2,1)} %get-tuple-element.276) | copy-start | bytes 393220 | tf_op jit(solution)/shard_map/while/body/eval_jaxpr/cond
  79.4 9.6 %copy-start.9 = (s32[128,8]{0,1:T(8,128)S(1)}, s32[128,8]{0,1:T(8,128)}, u32[]{:S(2)}) copy-start(s32[128,8]{0,1:T(8,128)} %param.29) | copy-start | bytes 12292
  88.9 2.7 copy-start.10
  89.6 0.7 copy-start.5
  90.4 57.8 %copy-start = (bf16[128,4096]{1,0:T(8,128)(2,1)S(1)}, bf16[128,4096]{1,0:T(8,128)(2,1)}, u32[]{:S(2)}) copy-start(bf16[128,4096]{1,0:T(8,128)(2,1)} %param.27) | copy-start | bytes 3145732
  94.0 57.1 %copy-start.8 = (f32[4096]{0:T(1024)S(1)}, f32[4096]{0:T(1024)}, u32[]{:S(2)}) copy-start(f32[4096]{0:T(1024)} %param.28) | copy-start | bytes 49156
Sparse Core Ops, SparseCore 0:
  9.5 69.8 all-gather.1
  89.1 59.0 reduce-scatter.1

commit v2 on v1

--- a/solution.py
+++ b/solution.py
@@ -8,7 +8,8 @@
 from jax.sharding import PartitionSpec as P
 
 HEAD_DIM = 128
-DOC_SHARDS = 4
+SHARD = 512
+BACK = 2048
 NEG_FILL = -1e30
 D = 4096
 HALF = D // 2
@@ -257,114 +258,292 @@
     )(normed, hidden, picks, gates, perm, perm_t, w_gate, w_up, w_down)
 
 
-def passed_along(x, axis, by):
-    count = lax.axis_size(axis)
-    pairs = [(i, i + by) for i in range(count) if 0 <= i + by < count]
-    return lax.ppermute(x, axis, pairs)
-
-
-def doc_index(positions, doc_ends):
-    return jnp.sum((positions[:, None] >= doc_ends[None, :]).astype(jnp.int32), axis=1)
-
-
-def body(
-    queries,
-    keys,
-    values,
-    doc_lengths,
-    out_weight,
-    residual,
-    norm_gain,
-    expert_ids,
-    gate_values,
-    w_gate,
-    w_up,
-    w_down,
+def rotated(chip, by):
+    return (chip + by + 16) % 16
+
+
+def chip_device(chip, c, z):
+    return device(chip // 4, chip % 4, c, z)
+
+
+def remote(src, dst, send_sem, recv_sem, target):
+    return pltpu.make_async_remote_copy(
+        src_ref=src, dst_ref=dst, send_sem=send_sem, recv_sem=recv_sem,
+        device_id=target, device_id_type=MESH,
+    )
+
+
+def wait_bytes(ref, sem):
+    pltpu.make_async_copy(ref, ref, sem).wait()
+
+
+def front_kernel(
+    doc_lengths, queries, keys, values, out_weight, residual, gain, normed, hidden,
+    kv, weight, att, relay, stage, fin,
+    kv_send, kv_recv, line_recv, line_fwd, plane_recv, plane_fwd, weight_send,
+    att_send, att_recv, relay_recv, fin_recv, term_send,
 ):
-    row_count = queries.shape[0]
-    kv_local = keys.shape[1] // HEAD_DIM
-    group = queries.shape[1] // keys.shape[1]
-    scale = HEAD_DIM ** (-0.5)
-    doc_ends = jnp.cumsum(doc_lengths)
-    my_start = lax.axis_index("seq") * row_count
-    query_pos = my_start + jnp.arange(row_count, dtype=jnp.int32)
-    query_doc = doc_index(query_pos, doc_ends)
-    query_heads = queries.reshape(row_count, kv_local, group, HEAD_DIM)
-
-    def attend_part(running, key_part, value_part, first):
-        width = key_part.shape[0]
-        key_pos = first + jnp.arange(width, dtype=jnp.int32)
-        key_doc = doc_index(key_pos, doc_ends)
-        visible = (
-            (key_pos[None, :] >= 0)
-            & (key_pos[None, :] <= query_pos[:, None])
-            & (key_doc[None, :] == query_doc[:, None])
-        )
-
-        def update(state):
-            top_old, total_old, accum_old = state
-            scores = (
-                jnp.einsum(
-                    "tkgd,skd->kgts",
-                    query_heads,
-                    key_part.reshape(width, kv_local, HEAD_DIM),
-                    preferred_element_type=jnp.float32,
-                )
-                * scale
+    y, x, c, z = place()
+    chip = y * 4 + x
+    partner = device(y, x, 1 - c, z)
+
+    def kv_slot(slot):
+        return kv.at[pl.ds(pl.multiple_of(slot * SHARD, SHARD), SHARD)]
+
+    own = pl.ds(pl.multiple_of((4 + c) * SHARD, SHARD), SHARD)
+    kv[own, 0:HEAD_DIM] = keys[...]
+    kv[own, HEAD_DIM : 2 * HEAD_DIM] = values[...]
+    for ahead in (1, 2):
+        remote(
+            kv_slot(4 + c), kv_slot(4 - 2 * ahead + c), kv_send, kv_recv.at[ahead - 1],
+            chip_device(rotated(chip, ahead), c, z),
+        ).start()
+
+    def spot(half, u, v):
+        return 4 * v + u if half == 0 else 4 * u + v
+
+    def spot_device(half, u, v):
+        return device(v, u, c, z) if half == 0 else device(u, v, c, z)
+
+    def cut(half, first, count, k, width=1):
+        lanes = pl.ds(pl.multiple_of(k * HEAD_DIM, HEAD_DIM), width * HEAD_DIM)
+        return weight.at[pl.ds(half * 512 + first, count), lanes]
+
+    home = ((x, y), (y, x))
+    weight[:, pl.ds(pl.multiple_of(chip * HEAD_DIM, HEAD_DIM), HEAD_DIM)] = out_weight[...]
+
+    def spread(half, u):
+        v = home[half][1]
+        block = cut(half, 0, 512, spot(half, u, v))
+        for way, step in enumerate((1, 3)):
+            remote(
+                block, block, weight_send, plane_recv.at[half, way],
+                spot_device(half, home[half][0], (v + step) % 4),
+            ).start()
+
+    for half in (0, 1):
+        u, v = home[half]
+        block = cut(half, 0, 512, spot(half, u, v))
+        for way, step in enumerate((1, 3)):
+            remote(
+                block, block, weight_send, line_recv.at[half, way],
+                spot_device(half, (u + step) % 4, v),
+            ).start()
+    for half in (0, 1):
+        spread(half, home[half][0])
+
+    def line_step():
+        for half in (0, 1):
+            u, v = home[half]
+            for way, step in enumerate((1, 3)):
+                wait_bytes(cut(half, 0, 512, 0), line_recv.at[half, way])
+                came = (u - step + 4) % 4
+                part = cut(half, 256 * way, 256, spot(half, came, v))
+                remote(
+                    part, part, weight_send, line_fwd.at[half, way],
+                    spot_device(half, (u + step) % 4, v),
+                ).start()
+                spread(half, came)
+
+    def line_end():
+        for half in (0, 1):
+            for way in (0, 1):
+                wait_bytes(cut(half, 0, 256, 0), line_fwd.at[half, way])
+            spread(half, (home[half][0] + 2) % 4)
+
+    def plane_step():
+        for half in (0, 1):
+            u, v = home[half]
+            for way, step in enumerate((1, 3)):
+                wait_bytes(cut(half, 0, 512, 0, 4), plane_recv.at[half, way])
+                came = (v - step + 4) % 4
+                target = spot_device(half, u, (v + step) % 4)
+                if half == 0:
+                    parts = [cut(half, 256 * way, 256, 4 * came, 4)]
+                else:
+                    parts = [cut(half, 256 * way, 256, spot(half, i, came)) for i in range(4)]
+                for part in parts:
+                    remote(part, part, weight_send, plane_fwd.at[half, way], target).start()
+
+    def plane_end():
+        for half in (0, 1):
+            for way in (0, 1):
+                wait_bytes(cut(half, 0, 256, 0, 4), plane_fwd.at[half, way])
+
+    for k in (0, 1):
+        wait_bytes(kv_slot(0), kv_recv.at[k])
+    for k, slot in enumerate((jnp.where(c == 0, 4, 1), 2 + c)):
+        remote(kv_slot(slot), kv_slot(slot), kv_send, kv_recv.at[2 + k], partner).start()
+    line_step()
+    for k in (2, 3):
+        wait_bytes(kv_slot(0), kv_recv.at[k])
+
+    ends = []
+    total_len = doc_lengths[0]
+    for i in range(doc_lengths.shape[0]):
+        if i:
+            total_len = total_len + doc_lengths[i]
+        ends.append(total_len)
+    factor = HEAD_DIM ** (-0.5) * 1.4426950408889634
+
+    def attend(b, carry):
+        base = pl.multiple_of(512 * c + 128 * b, 128)
+        first = (chip * 2 + c) * SHARD + b * 128
+        pos = first + lax.broadcasted_iota(jnp.int32, (128, 1), 0)
+        low = jnp.zeros((128, 1), jnp.int32)
+        for end in ends:
+            low = jnp.where(pos >= end, end, low)
+        low = low - (first - BACK)
+        low = jnp.concatenate([low, low], axis=0)
+
+        def heads(hp, carry):
+            lanes = pl.multiple_of(hp * 256, 256)
+            both = queries[pl.ds(pl.multiple_of(b * 128, 128), 128), pl.ds(lanes, 256)]
+            q = jnp.concatenate([both[:, 0:128], both[:, 128:256]], axis=0)
+            nt = (((1,), (1,)), ((), ()))
+            far = lax.dot_general(
+                q, kv[pl.ds(base, BACK), 0:HEAD_DIM], nt, preferred_element_type=jnp.float32
             )
-            masked = jnp.where(visible, scores, NEG_FILL)
-            top_new = jnp.maximum(top_old, jnp.max(masked, axis=-1))
-            factor = jnp.exp(top_old - top_new)
-            weights = jnp.where(visible, jnp.exp(masked - top_new[..., None]), 0.0)
-            total_new = total_old * factor + jnp.sum(weights, axis=-1)
-            added = jnp.einsum(
-                "kgts,skd->kgtd",
-                weights.astype(jnp.bfloat16),
-                value_part.reshape(width, kv_local, HEAD_DIM),
+            near = lax.dot_general(
+                q, kv[pl.ds(base + BACK, 128), 0:HEAD_DIM], nt,
                 preferred_element_type=jnp.float32,
             )
-            return (top_new, total_new, accum_old * factor[..., None] + added)
-
-        return lax.cond(jnp.any(visible), update, lambda state: state, running)
-
-    def absorb(running, shards, offset):
-        key_all, value_all = shards
-        width = key_all.shape[0]
-        step_len = width
-
-        def inner(index, state):
-            begin = index * step_len
-            return attend_part(state, key_all, value_all, offset + begin)
-
-        return lax.fori_loop(0, width // step_len, inner, running)
-
-    start_top = jnp.full((kv_local, group, row_count), NEG_FILL, jnp.float32)
-    start_total = jnp.zeros((kv_local, group, row_count), jnp.float32)
-    start_accum = jnp.zeros((kv_local, group, row_count, HEAD_DIM), jnp.float32)
-    initial = (start_top, start_total, start_accum)
-    final_state = absorb(initial, (keys, values), my_start)
-    for distance in range(1, DOC_SHARDS + 1):
-        earlier = passed_along((keys, values), "seq", distance)
-        final_state = absorb(final_state, earlier, my_start - distance * row_count)
-    top_last, total_last, accum_last = final_state
-    attended = accum_last / total_last[..., None]
-    attended = (
-        jnp.transpose(attended, (2, 0, 1, 3))
-        .reshape(row_count, kv_local * group * HEAD_DIM)
-        .astype(jnp.bfloat16)
-    )
-    partial_terms = jnp.dot(
-        attended,
-        lax.all_gather(out_weight, "seq", axis=1, tiled=True),
-        preferred_element_type=jnp.float32,
-    )
-    projected = lax.psum_scatter(
-        partial_terms.astype(jnp.bfloat16), "exp", scatter_dimension=0, tiled=True
-    ).astype(jnp.float32)
-    hidden_state = residual.astype(jnp.float32) + projected
-    variance = jnp.mean(hidden_state * hidden_state, axis=1, keepdims=True)
-    normed = (hidden_state * lax.rsqrt(variance + 1e-06) * norm_gain[None, :]).astype(jnp.bfloat16)
-    return routed_layer(normed, hidden_state, expert_ids, gate_values, w_gate, w_up, w_down)
+            at = lax.broadcasted_iota(jnp.int32, (256, BACK), 1)
+            far = jnp.where(at >= low, far, NEG_FILL)
+            at = lax.broadcasted_iota(jnp.int32, (256, 128), 1)
+            row = lax.broadcasted_iota(jnp.int32, (256, 128), 0) % 128
+            near = jnp.where((at + BACK >= low) & (at <= row), near, NEG_FILL)
+            top = jnp.maximum(
+                jnp.max(far, axis=1, keepdims=True), jnp.max(near, axis=1, keepdims=True)
+            )
+            far = jnp.exp2((far - top) * factor)
+            near = jnp.exp2((near - top) * factor)
+            total = jnp.sum(far, axis=1, keepdims=True) + jnp.sum(near, axis=1, keepdims=True)
+            got = jnp.dot(
+                far.astype(jnp.bfloat16), kv[pl.ds(base, BACK), HEAD_DIM : 2 * HEAD_DIM],
+                preferred_element_type=jnp.float32,
+            ) + jnp.dot(
+                near.astype(jnp.bfloat16),
+                kv[pl.ds(base + BACK, 128), HEAD_DIM : 2 * HEAD_DIM],
+                preferred_element_type=jnp.float32,
+            )
+            got = (got / total).astype(jnp.bfloat16)
+            att[b, c, :, pl.ds(lanes, 256)] = jnp.concatenate([got[0:128], got[128:256]], axis=1)
+            return carry
+
+        lax.fori_loop(0, 4, heads, 0)
+        remote(att.at[b, c], att.at[b, c], att_send, att_recv, partner).start()
+        pl.when(b == 0)(line_end)
+        pl.when(b == 2)(plane_step)
+        return carry
+
+    lax.fori_loop(0, 4, attend, 0)
+    plane_end()
+    wait_bytes(stage.at[pl.ds(0, 4)], att_recv)
+
+    def terms(tz, half):
+        return jnp.dot(
+            att[tz].reshape(256, 1024), weight[:, half * 1024 : (half + 1) * 1024],
+            preferred_element_type=jnp.float32,
+        )
+
+    def put(step, half, value):
+        at = (step * 2 + half) * 2
+        stage[at : at + 2] = value.astype(jnp.bfloat16).reshape(2, 128, 1024)
+        return at
+
+    up, down = (z + 1) % 4, (z + 3) % 4
+    far_z = (z + 2) % 4
+    for half, nearer in enumerate((up, down)):
+        at = put(0, half, terms(far_z, half))
+        remote(
+            stage.at[pl.ds(at, 2)], relay.at[half], term_send, relay_recv.at[half],
+            device(y, x, c, nearer),
+        ).start()
+
+    def deliver(side, half, tz, at):
+        for tc in (0, 1):
+            remote(
+                stage.at[at + tc], fin.at[(side * 2 + c) * 2 + half], term_send, fin_recv,
+                device(y, x, tc, tz),
+            ).start()
+
+    deliver(0, 1, up, put(1, 1, terms(up, 1)))
+    deliver(1, 0, down, put(2, 0, terms(down, 0)))
+    for half in (0, 1):
+        at = put(3, half, terms(z, half))
+        spot_at = (2 * 2 + c) * 2 + half
+        fin[spot_at] = stage[at + c]
+        remote(stage.at[at + 1 - c], fin.at[spot_at], term_send, fin_recv, partner).start()
+    for half, tz in enumerate((up, down)):
+        value = terms(tz, half)
+        wait_bytes(relay.at[half], relay_recv.at[half])
+        value = value + relay[half].reshape(256, 1024).astype(jnp.float32)
+        deliver(half, half, tz, put(1 + half, half, value))
+
+    wait_bytes(fin.at[pl.ds(0, 10)], fin_recv)
+    squares = jnp.zeros((128, HEAD_DIM), jnp.float32)
+    for cs in (0, 1):
+        for k in range(16):
+            half, kk = k // 8, k % 8
+            lanes = slice((2 * k + cs) * 128, (2 * k + cs + 1) * 128)
+            value = residual[:, lanes].astype(jnp.float32)
+            for side in range(3):
+                value = value + fin[
+                    (side * 2 + cs) * 2 + half, :, kk * 128 : (kk + 1) * 128
+                ].astype(jnp.float32)
+            hidden[:, lanes] = value
+            squares = squares + value * value
+    variance = jnp.sum(squares, axis=1, keepdims=True) * (1.0 / D)
+    shrink = lax.rsqrt(variance + 1e-06)
+    for first in range(0, D, CHUNK):
+        lanes = slice(first, first + CHUNK)
+        normed[:, lanes] = (hidden[:, lanes] * shrink * gain[:, lanes]).astype(jnp.bfloat16)
+
+    for _ in range(4):
+        wait_bytes(kv_slot(0), kv_send)
+    wait_bytes(weight.at[:, 0:1920], weight_send)
+    wait_bytes(stage.at[pl.ds(0, 4)], att_send)
+    wait_bytes(stage.at[pl.ds(0, 14)], term_send)
+
+
+def front(queries, keys, values, doc_lengths, out_weight, residual, norm_gain):
+    vmem = pl.BlockSpec(memory_space=pltpu.VMEM)
+    dma = pltpu.SemaphoreType.DMA
+    tokens = residual.shape[0]
+    return pl.pallas_call(
+        front_kernel,
+        out_shape=(
+            jax.ShapeDtypeStruct((tokens, D), jnp.bfloat16),
+            jax.ShapeDtypeStruct((tokens, D), jnp.float32),
+        ),
+        in_specs=[pl.BlockSpec(memory_space=pltpu.SMEM)] + [vmem] * 6,
+        out_specs=(vmem, vmem),
+        scratch_shapes=[
+            pltpu.VMEM((6 * SHARD, 2 * HEAD_DIM), jnp.bfloat16),
+            pltpu.VMEM((1024, HALF), jnp.bfloat16),
+            pltpu.VMEM((4, 2, 128, 1024), jnp.bfloat16),
+            pltpu.VMEM((2, 2, 128, 1024), jnp.bfloat16),
+            pltpu.VMEM((16, 128, 1024), jnp.bfloat16),
+            pltpu.VMEM((12, 128, 1024), jnp.bfloat16),
+            dma, dma((4,)), dma((2, 2)), dma((2, 2)), dma((2, 2)), dma((2, 2)), dma,
+            dma, dma, dma((2,)), dma, dma,
+        ],
+        compiler_params=pltpu.CompilerParams(
+            has_side_effects=True, vmem_limit_bytes=60 * 1024 * 1024
+        ),
+        cost_estimate=pl.CostEstimate(
+            flops=10**10, bytes_accessed=10**7, transcendentals=10**7
+        ),
+    )(doc_lengths, queries, keys, values, out_weight, residual, norm_gain.reshape(1, D))
+
+
+def body(
+    queries, keys, values, doc_lengths, out_weight, residual, norm_gain, expert_ids,
+    gate_values, w_gate, w_up, w_down,
+):
+    normed, hidden = front(queries, keys, values, doc_lengths, out_weight, residual, norm_gain)
+    return routed_layer(normed, hidden, expert_ids, gate_values, w_gate, w_up, w_down)
 
 
 def solution(mesh):

time: 409 us -> 347 us (0.85)
  the two profiles are of different devices: /device:TPU:1 before, /device:TPU:38 now
where the time goes in v2:
time: 347 us; the launch traced here: 342 us
  Pallas kernels  332 us (96%)
  other arithmetic  5.35 us (2%)
  local copies, waits for them, and re-layouts  4.17 us (1%)
    pallas_call x1, Pallas kernels, routed_layer(): pl.pallas_call(moe_kernel, out_shape=jax.ShapeDtypeStruct((tokens, D), jn...  238 us
    pallas_call x1, Pallas kernels, front(): pl.pallas_call(front_kernel, out_shape=(jax.ShapeDtypeStruct((tokens, D),...  94 us

profile of v2, /device:TPU:38, one launch (start us, length us, event | category | flops | bytes accessed | tf_op | source)
XLA Modules:
  0.0 341.7 jit_solution(10067033047899791902)
XLA Ops:
  0.1 0.9 compare_reduce_fusion
  1.0 0.1 convolution_select_fusion
  1.1 0.9 fusion.4
  2.1 0.1 copy.21
  2.2 0.1 copy.24
  2.3 1.1 fusion.3
  3.5 0.3 fusion.1
  3.8 0.1 slice.16
  4.0 0.4 copy.22
  4.3 0.1 copy.23
  4.4 0.7 pad_maximum_fusion.picks
  5.2 0.3 fusion
  5.5 0.2 slice.18
  5.7 0.6 copy.25
  6.3 0.2 copy.26
  6.5 0.9 maximum_bitcast_fusion.gates
  7.5 94.0 %shard_map.118 = (bf16[128,4096]{1,0:T(8,128)(2,1)}, f32[128,4096]{1,0:T(8,128)}) custom-call(s32[16]{0:T(128)} %doc_lengths.1, bf16[512,1024]{1,0:T(8,128)(2,1)} %queries.1, bf16[512,128]{1,0:T(8,128)(2,1)} %keys.1, bf16[512,128]{1,0:T(8,128)(2,1)} %values.1, bf16[1024,128]{1,0:T(8,128)(2,1)} %out_weight.1, bf16[128,4096]{1,0:T(8,128)(2,1)} %residual.1, ...), custom_call_target="tpu_custom_call" | custom-call | flops 10000000000 | bytes 10000000 | tf_op jit(solution)/shard_map/pallas_call | solution.py:514
  101.5 238.0 %shard_map.119 = bf16[128,4096]{1,0:T(8,128)(2,1)} custom-call(bf16[128,4096]{1,0:T(8,128)(2,1)} %get-tuple-element.7.normed, f32[128,4096]{1,0:T(8,128)} %get-tuple-element.8.hidden, bf16[4,288,128]{2,1,0:T(8,128)(2,1)} %pad_maximum_fusion.picks, f32[4,128,288]{2,1,0:T(8,128)} %maximum_bitcast_fusion.gates, bf16[512,512]{1,0:T(8,128)(2,1)} %get-tuple-element.10.perm, ...), custom_call_target="tpu_custom_call" | custom-call | flops 24000000000 | bytes 40000000 | tf_op jit(solution)/shard_map/pallas_call | solution.py:231
  339.4 2.3 copy.28
  (4 shorter events, 0.1 us)

commit v3 on v2

v3 whole, which is shorter than its diff:
```python
import functools

import jax
import jax.numpy as jnp
from jax import lax
from jax.experimental import pallas as pl
from jax.experimental.pallas import tpu as pltpu
from jax.sharding import PartitionSpec as P

HEAD_DIM = 128
SHARD = 512
NEG_FILL = -1e30
D = 4096
HALF = D // 2
FFH = 768
CAP = 9
TOPK = 8
DEVICES = 128
GROUPS = 4
PER_GROUP = DEVICES // GROUPS
MAIN = PER_GROUP * 8
ROWS = PER_GROUP * CAP
EXTRA = D // 16
MESSAGE = HALF + EXTRA
CHUNK = 512
STRIDE = 37
MESH = pl.DeviceIdType.MESH


def place():
    seq = lax.axis_index("seq")
    return seq // 8, (seq // 2) % 4, seq % 2, lax.axis_index("exp")


def device(y, x, c, z):
    return {"seq": (y * 4 + x) * 2 + c, "exp": z}


def route_target(index):
    y, x, c, z = place()
    j = (index * STRIDE) % DEVICES
    dy, dx, dc, dz = j // 32, (j // 8) % 4, (j // 4) % 2, j % 4
    ey = jnp.where(c == 0, dy, dx)
    ex = jnp.where(c == 0, dx, dz)
    ez = jnp.where(c == 0, dz, dy)
    return (y + ey) % 4, (x + ex) % 4, (c + dc) % 2, (z + ez) % 4


def route_source(index):
    y, x, c, z = place()
    j = (index * STRIDE) % DEVICES
    dy, dx, dc, dz = j // 32, (j // 8) % 4, (j // 4) % 2, j % 4
    sc = (c + dc) % 2
    ey = jnp.where(sc == 0, dy, dx)
    ex = jnp.where(sc == 0, dx, dz)
    ez = jnp.where(sc == 0, dz, dy)
    return (y - ey + 4) % 4, (x - ex + 4) % 4, sc, (z - ez + 4) % 4


def target_ids(first):
    y, x, c, z = place()
    index = first + lax.broadcasted_iota(jnp.int32, (1, PER_GROUP), 1)
    j = (index * STRIDE) & (DEVICES - 1)
    dy, dx, dc, dz = j >> 5, (j >> 3) & 3, (j >> 2) & 1, j & 3
    ey = jnp.where(c == 0, dy, dx)
    ex = jnp.where(c == 0, dx, dz)
    ez = jnp.where(c == 0, dz, dy)
    ty, tx, tc, tz = (y + ey) & 3, (x + ex) & 3, (c + dc) & 1, (z + ez) & 3
    return (((ty * 4 + tx) * 2 + tc) * 4 + tz).astype(jnp.float32)


def slot_of(row):
    return jnp.where(row < MAIN, row >> 3, row - MAIN), jnp.where(row < MAIN, row & 7, 8)


def moe_kernel(
    normed, hidden, ids_t, gates_t, w_gate, w_up, w_down, out,
    outbound, arrived, returned, wg, wu, wd, rows, extra, acc, perm, posn, gate,
    weight_sem, hidden_sem, send_sem, recv_sem, back_send_sem, back_recv_sem,
):
    tokens = normed.shape[0]
    loads = [
        pltpu.make_async_copy(src.at[0], dst, weight_sem.at[k])
        for k, (src, dst) in enumerate(((w_gate, wg), (w_up, wu), (w_down, wd)))
    ]
    for load in loads:
        load.start()
    fetch = pltpu.make_async_copy(hidden, acc, hidden_sem)
    fetch.start()
    line = lax.broadcasted_iota(jnp.int32, (16 * PER_GROUP, 16 * PER_GROUP), 0)
    other = lax.broadcasted_iota(jnp.int32, (16 * PER_GROUP, 16 * PER_GROUP), 1)
    perm[...] = (other == (line & (PER_GROUP - 1)) * 16 + (line >> 5)).astype(jnp.bfloat16)

    def pack(buffer, first, c, left, right):
        both = jnp.concatenate(
            [left.reshape(PER_GROUP, 8, CHUNK), right.reshape(PER_GROUP, 8, CHUNK)], axis=1
        )
        buffer[pl.ds(first, PER_GROUP), :, c : c + CHUNK] = both.astype(jnp.bfloat16)

    def pack_extra(buffer, first):
        stacked = jnp.concatenate(
            [extra[:, j * EXTRA : (j + 1) * EXTRA] for j in range(16)], axis=0
        ).astype(jnp.bfloat16)
        turned = lax.dot_general(
            perm[...], stacked, (((0,), (0,)), ((), ())), preferred_element_type=jnp.float32
        )
        buffer[pl.ds(first, PER_GROUP), :, HALF:MESSAGE] = turned.astype(jnp.bfloat16).reshape(
            PER_GROUP, 16, EXTRA
        )

    def unpack(buffer, first):
        for c in range(0, HALF, CHUNK):
            both = buffer[pl.ds(first, PER_GROUP), :, c : c + CHUNK].astype(jnp.float32)
            rows[0:MAIN, c : c + CHUNK] = both[:, 0:8].reshape(MAIN, CHUNK).astype(jnp.bfloat16)
            rows[0:MAIN, HALF + c : HALF + c + CHUNK] = (
                both[:, 8:16].reshape(MAIN, CHUNK).astype(jnp.bfloat16)
            )
        stacked = buffer[pl.ds(first, PER_GROUP), :, HALF:MESSAGE].reshape(PER_GROUP * 16, EXTRA)
        turned = jnp.dot(perm[...], stacked, preferred_element_type=jnp.float32)
        for j in range(16):
            rows[MAIN:ROWS, j * EXTRA : (j + 1) * EXTRA] = turned[
                j * PER_GROUP : (j + 1) * PER_GROUP
            ].astype(jnp.bfloat16)

    routes = jnp.transpose(
        jnp.concatenate(
            [
                ids_t[...].astype(jnp.float32), gates_t[...],
                jnp.zeros((tokens - 2 * TOPK, tokens), jnp.float32),
            ],
            axis=0,
        )
    )
    earlier = (
        lax.broadcasted_iota(jnp.int32, (tokens, tokens), 0)
        > lax.broadcasted_iota(jnp.int32, (tokens, tokens), 1)
    ).astype(jnp.bfloat16)

    def build(q, carry):
        first = q * PER_GROUP
        target = target_ids(first)
        member = jnp.zeros((tokens, PER_GROUP), jnp.float32)
        weight = jnp.zeros((tokens, PER_GROUP), jnp.float32)
        for k in range(TOPK):
            hit = routes[:, k : k + 1] == target
            member = jnp.where(hit, 1.0, member)
            weight = jnp.where(hit, routes[:, TOPK + k : TOPK + k + 1], weight)
        count = jnp.dot(earlier, member.astype(jnp.bfloat16), preferred_element_type=jnp.float32)
        count = jnp.where(member > 0.0, count, -1.0)
        posn[q] = count
        gate[q] = weight
        row = lax.broadcasted_iota(jnp.int32, (ROWS, PER_GROUP), 0)
        message, _ = slot_of(row)
        spread = (message == lax.broadcasted_iota(jnp.int32, (ROWS, PER_GROUP), 1)).astype(
            jnp.bfloat16
        )
        picked = lax.dot_general(
            spread, count.astype(jnp.bfloat16), (((1,), (1,)), ((), ())),
            preferred_element_type=jnp.float32,
        )
        _, slot = slot_of(lax.broadcasted_iota(jnp.int32, (ROWS, tokens), 0))
        picks = (picked == slot.astype(jnp.float32)).astype(jnp.bfloat16)
        for c in range(0, HALF, CHUNK):
            halves = []
            for base in (c, HALF + c):
                got = jnp.dot(
                    picks, normed[:, base : base + CHUNK], preferred_element_type=jnp.float32
                )
                extra[:, base : base + CHUNK] = got[MAIN:ROWS]
                halves.append(got[0:MAIN])
            pack(outbound, first, c, *halves)
        pack_extra(outbound, first)

        def send(k, carry):
            index = first + k

            @pl.when(index == 0)
            def _():
                pltpu.make_async_copy(outbound.at[0], arrived.at[0], recv_sem.at[0]).start()

            @pl.when(index > 0)
            def _():
                pltpu.make_async_remote_copy(
                    src_ref=outbound.at[index],
                    dst_ref=arrived.at[index],
                    send_sem=send_sem,
                    recv_sem=recv_sem.at[q],
                    device_id=device(*route_target(index)),
                    device_id_type=MESH,
                ).start()

            return carry

        return lax.fori_loop(0, PER_GROUP, send, carry)

    lax.fori_loop(0, GROUPS, build, 0)
    for load in loads:
        load.wait()

    def expert(q, carry):
        first = q * PER_GROUP
        block = arrived.at[pl.ds(first, PER_GROUP)]
        pltpu.make_async_copy(block, block, recv_sem.at[q]).wait()
        unpack(arrived, first)
        gate_part = jnp.dot(rows[...], wg[...], preferred_element_type=jnp.float32)
        up_part = jnp.dot(rows[...], wu[...], preferred_element_type=jnp.float32)
        inner = (gate_part / (1.0 + jnp.exp(-gate_part)) * up_part).astype(jnp.bfloat16)
        for c in range(0, HALF, CHUNK):
            halves = []
            for base in (c, HALF + c):
                got = jnp.dot(
                    inner, wd[:, base : base + CHUNK], preferred_element_type=jnp.float32
                )
                extra[:, base : base + CHUNK] = got[MAIN:ROWS]
                halves.append(got[0:MAIN])
            pack(arrived, first, c, *halves)
        pack_extra(arrived, first)

        def send(k, carry):
            index = first + k

            @pl.when(index == 0)
            def _():
                pltpu.make_async_copy(arrived.at[0], returned.at[0], back_recv_sem.at[0]).start()

            @pl.when(index > 0)
            def _():
                pltpu.make_async_remote_copy(
                    src_ref=arrived.at[index],
                    dst_ref=returned.at[index],
                    send_sem=back_send_sem,
                    recv_sem=back_recv_sem.at[q],
                    device_id=device(*route_source(index)),
                    device_id_type=MESH,
                ).start()

            return carry

        return lax.fori_loop(0, PER_GROUP, send, carry)

    lax.fori_loop(0, GROUPS, expert, 0)
    row = lax.broadcasted_iota(jnp.int32, (PER_GROUP, ROWS), 1)
    message, _ = slot_of(row)
    gather = (message == lax.broadcasted_iota(jnp.int32, (PER_GROUP, ROWS), 0)).astype(jnp.bfloat16)
    _, slot = slot_of(lax.broadcasted_iota(jnp.int32, (tokens, ROWS), 1))
    slot = slot.astype(jnp.float32)

    def combine(q, carry):
        first = q * PER_GROUP
        block = returned.at[pl.ds(first, PER_GROUP)]
        pltpu.make_async_copy(block, block, back_recv_sem.at[q]).wait()
        unpack(returned, first)
        spread = functools.partial(jnp.dot, preferred_element_type=jnp.float32)
        used = spread(posn[q].astype(jnp.bfloat16), gather) == slot
        high = gate[q].astype(jnp.bfloat16)
        low = (gate[q] - high.astype(jnp.float32)).astype(jnp.bfloat16)
        both = jnp.concatenate(
            [jnp.where(used, spread(half, gather), 0.0) for half in (high, low)], axis=0
        ).astype(jnp.bfloat16)
        for c in range(0, D, CHUNK):
            got = jnp.dot(both, rows[:, c : c + CHUNK], preferred_element_type=jnp.float32)
            acc[:, c : c + CHUNK] += got[0:tokens] + got[tokens : 2 * tokens]
        return carry

    fetch.wait()
    lax.fori_loop(0, GROUPS, combine, 0)
    out[...] = acc[...].astype(jnp.bfloat16)
    sent = outbound.at[pl.ds(1, DEVICES - 1)]
    for sem in (send_sem, back_send_sem):
        pltpu.make_async_copy(sent, sent, sem).wait()


def routed_layer(normed, hidden, expert_ids, gate_values, w_gate, w_up, w_down):
    tokens = normed.shape[0]
    vmem = pl.BlockSpec(memory_space=pltpu.VMEM)
    anywhere = pl.BlockSpec(memory_space=pl.ANY)
    dma = pltpu.SemaphoreType.DMA
    messages = pltpu.VMEM((DEVICES, 16, MESSAGE), jnp.bfloat16)
    return pl.pallas_call(
        moe_kernel,
        out_shape=jax.ShapeDtypeStruct((tokens, D), jnp.bfloat16),
        in_specs=[vmem, anywhere, vmem, vmem] + [anywhere] * 3,
        out_specs=vmem,
        scratch_shapes=[
            messages, messages, messages,
            pltpu.VMEM((D, FFH), jnp.bfloat16),
            pltpu.VMEM((D, FFH), jnp.bfloat16),
            pltpu.VMEM((FFH, D), jnp.bfloat16),
            pltpu.VMEM((ROWS, D), jnp.bfloat16),
            pltpu.VMEM((PER_GROUP, D), jnp.float32),
            pltpu.VMEM((tokens, D), jnp.float32),
            pltpu.VMEM((16 * PER_GROUP, 16 * PER_GROUP), jnp.bfloat16),
            pltpu.VMEM((GROUPS, tokens, PER_GROUP), jnp.float32),
            pltpu.VMEM((GROUPS, tokens, PER_GROUP), jnp.float32),
            dma((3,)), dma, dma, dma((GROUPS,)), dma, dma((GROUPS,)),
        ],
        compiler_params=pltpu.CompilerParams(
            has_side_effects=True, vmem_limit_bytes=64 * 1024 * 1024
        ),
        cost_estimate=pl.CostEstimate(
            flops=24 * 10**9, bytes_accessed=40 * 10**6, transcendentals=10**6
        ),
    )(normed, hidden, expert_ids.T, gate_values.T, w_gate, w_up, w_down)


def rotated(chip, by):
    return (chip + by) % 16


def chip_device(chip, c, z):
    return device(chip // 4, chip % 4, c, z)


def remote(src, dst, send_sem, recv_sem, target):
    return pltpu.make_async_remote_copy(
        src_ref=src, dst_ref=dst, send_sem=send_sem, recv_sem=recv_sem,
        device_id=target, device_id_type=MESH,
    )


def wait_bytes(ref, sem):
    pltpu.make_async_copy(ref, ref, sem).wait()


def front_kernel(
    doc_lengths, queries, keys, values, out_weight, residual, gain, normed, hidden,
    kv, weight, att, relay, stage, fin, tops, totals, sums,
    kv_send, kv_recv, line_recv, line_fwd, plane_recv, plane_fwd, weight_send,
    att_send, att_recv, relay_recv, fin_recv, term_send,
):
    y, x, c, z = place()
    chip = y * 4 + x
    partner = device(y, x, 1 - c, z)
    barrier = pltpu.get_barrier_semaphore()
    peers = [partner]
    for by in (1, 2, 14, 15):
        peers.append(chip_device(rotated(chip, by), c, z))
    for by in (1, 3):
        peers.append(device(y, (x + by) % 4, c, z))
        peers.append(device((y + by) % 4, x, c, z))
        peers.append(device(y, x, c, (z + by) % 4))
        peers.append(device(y, x, 1 - c, (z + by) % 4))
    for peer in peers:
        pl.semaphore_signal(barrier, inc=1, device_id=peer, device_id_type=MESH)
    pl.semaphore_wait(barrier, len(peers))

    def kv_slot(slot):
        return kv.at[pl.ds(pl.multiple_of(slot * SHARD, SHARD), SHARD)]

    weight[chip] = out_weight[...]

    def spread(u):
        block = weight.at[4 * y + u]
        for way, step in enumerate((1, 3)):
            remote(
                block, block, weight_send, plane_recv.at[way], device((y + step) % 4, x, c, z)
            ).start()

    for way, step in enumerate((1, 3)):
        block = weight.at[chip]
        remote(
            block, block, weight_send, line_recv.at[way], device(y, (x + step) % 4, c, z)
        ).start()
    spread(x)
    own = pl.ds(pl.multiple_of((4 + c) * SHARD, SHARD), SHARD)
    kv[own, 0:HEAD_DIM] = keys[...]
    kv[own, HEAD_DIM : 2 * HEAD_DIM] = values[...]
    for ahead in (1, 2):
        remote(
            kv_slot(4 + c), kv_slot(4 - 2 * ahead + c), kv_send, kv_recv.at[ahead - 1],
            chip_device(rotated(chip, ahead), c, z),
        ).start()

    def line_step():
        for way, step in enumerate((1, 3)):
            wait_bytes(weight.at[0], line_recv.at[way])
            came = (x - step + 4) % 4
            part = weight.at[4 * y + came, pl.ds(512 * way, 512)]
            remote(
                part, part, weight_send, line_fwd.at[way], device(y, (x + step) % 4, c, z)
            ).start()
            spread(came)

    def line_end():
        for way in (0, 1):
            wait_bytes(weight.at[0, pl.ds(0, 512)], line_fwd.at[way])
        spread((x + 2) % 4)

    def plane_step(way):
        step = (1, 3)[way]
        wait_bytes(weight.at[pl.ds(0, 4)], plane_recv.at[way])
        came = (y - step + 4) % 4
        part = weight.at[pl.ds(4 * came, 4), pl.ds(512 * way, 512)]
        remote(
            part, part, weight_send, plane_fwd.at[way], device((y + step) % 4, x, c, z)
        ).start()

    def plane_end():
        for way in (0, 1):
            wait_bytes(weight.at[pl.ds(0, 4), pl.ds(0, 512)], plane_fwd.at[way])

    def hand_over(slot, sem):
        remote(kv_slot(slot), kv_slot(slot), kv_send, kv_recv.at[sem], partner).start()

    pl.when(c == 0)(lambda: hand_over(4, 2))
    ends = []
    total_len = doc_lengths[0]
    for i in range(doc_lengths.shape[0]):
        if i:
            total_len = total_len + doc_lengths[i]
        ends.append(total_len)
    factor = HEAD_DIM ** (-0.5) * 1.4426950408889634

    def row_of(j):
        return (y + (0, 3, 1, 2)[j]) % 4

    def term(i, j):
        columns = [weight[4 * row_of(j) + u] for u in range(4)]
        return jnp.dot(
            att[i].reshape(256, 1024), jnp.concatenate(columns, axis=1),
            preferred_element_type=jnp.float32,
        )

    def put(i, j, value):
        at = (i * 4 + row_of(j)) * 2
        stage[pl.ds(at, 2)] = value.astype(jnp.bfloat16).reshape(2, 128, 512)
        return at

    up, down = (z + 1) % 4, (z + 3) % 4

    def deliver(i, j, value):
        at = put(i, j, value)
        for tc in (0, 1):
            remote(
                stage.at[at + tc], fin.at[((i - 1) * 2 + c) * 4 + row_of(j)], term_send, fin_recv,
                device(y, x, tc, (up, down)[i - 1]),
            ).start()

    def relay_out(j):
        at = put(0, j, term(0, j))
        remote(
            stage.at[pl.ds(at, 2)], relay.at[pl.ds(2 * row_of(j), 2)], term_send, relay_recv.at[j],
            device(y, x, c, (up, down)[j % 2]),
        ).start()

    def direct(i, j):
        deliver(i, j, term(i, j))

    def relayed(i, j):
        value = term(i, j)
        wait_bytes(relay.at[pl.ds(0, 2)], relay_recv.at[j])
        passed = relay[pl.ds(2 * row_of(j), 2)].reshape(256, 512)
        deliver(i, j, value + passed.astype(jnp.float32))

    def keep(j):
        at = put(3, j, term(3, j))
        spot = (4 + c) * 4 + row_of(j)
        fin[spot] = stage[at + c]
        remote(stage.at[at + 1 - c], fin.at[spot], term_send, fin_recv, partner).start()

    def after_far():
        wait_bytes(stage.at[pl.ds(0, 2)], att_recv.at[0])
        relay_out(0)
        plane_step(0)
        plane_step(1)
        relay_out(1)
        relay_out(2)

    def after_up():
        wait_bytes(stage.at[pl.ds(0, 2)], att_recv.at[1])
        relayed(1, 0)
        direct(1, 1)

    def after_down():
        wait_bytes(stage.at[pl.ds(0, 2)], att_recv.at[2])
        direct(2, 0)
        direct(2, 2)
        relayed(2, 1)
        relayed(1, 2)

    def after_own():
        wait_bytes(stage.at[pl.ds(0, 2)], att_recv.at[3])
        plane_end()
        relay_out(3)
        direct(1, 3)
        for j in range(4):
            keep(j)
        relayed(2, 3)

    def attend(slots, first, last):
        held = [kv_slot(slot) for slot in slots]
        starts = [(chip - 2) * 2 * SHARD + slot * SHARD for slot in slots]

        def block(i, carry):
            b = (z + jnp.where(i == 2, 3, jnp.where(i == 3, 0, 2 - i))) % 4
            pos = (chip * 2 + c) * SHARD + b * 128 + lax.broadcasted_iota(jnp.int32, (128, 1), 0)
            low = jnp.zeros((128, 1), jnp.int32)
            for end in ends:
                low = jnp.where(pos >= end, end, low)
            low = jnp.concatenate([low, low], axis=0)
            high = jnp.concatenate([pos, pos], axis=0)

            def heads(hp):
                n = i * 4 + hp
                lanes = hp * 256
                both = queries[pl.ds(pl.multiple_of(b * 128, 128), 128), pl.ds(lanes, 256)]
                q = jnp.concatenate([both[:, 0:128], both[:, 128:256]], axis=0)
                at = lax.broadcasted_iota(jnp.int32, (256, SHARD), 1)
                scores, top = [], None
                for ref, start in zip(held, starts):
                    part = lax.dot_general(
                        q, ref[:, 0:HEAD_DIM], (((1,), (1,)), ((), ())),
                        preferred_element_type=jnp.float32,
                    )
                    seen = at >= low - start
                    if first:
                        seen = seen & (at <= high - start)
                    part = jnp.where(seen, part, NEG_FILL)
                    peak = jnp.max(part, axis=1, keepdims=True)
                    top = peak if top is None else jnp.maximum(top, peak)
                    scores.append(part)
                if not first:
                    old = tops[n][:, 0:1]
                    top = jnp.maximum(top, old)
                    shrink = jnp.exp2((old - top) * factor)
                    total = totals[n][:, 0:1] * shrink
                    got = sums[n] * shrink
                for part, ref in zip(scores, held):
                    weights = jnp.exp2((part - top) * factor)
                    more = jnp.sum(weights, axis=1, keepdims=True)
                    value = jnp.dot(
                        weights.astype(jnp.bfloat16), ref[:, HEAD_DIM : 2 * HEAD_DIM],
                        preferred_element_type=jnp.float32,
                    )
                    if first:
                        total, got = more, value
                    else:
                        total, got = total + more, got + value
                if not last:
                    tops[n] = jnp.broadcast_to(top, (256, 128))
                    totals[n] = jnp.broadcast_to(total, (256, 128))
                    sums[n] = got
                else:
                    got = (got / total).astype(jnp.bfloat16)
                    att[i, c, :, pl.ds(lanes, 256)] = jnp.concatenate(
                        [got[0:128], got[128:256]], axis=1
                    )

            for hp in range(4):
                heads(hp)
                if last and hp == 1:
                    for k, then in enumerate((after_far, after_up, after_down)):
                        pl.when(i == k + 1)(then)
            if last:
                remote(att.at[i, c], att.at[i, c], att_send, att_recv.at[i], partner).start()
            return carry

        lax.fori_loop(0, 4, block, 0)

    attend([4 + c], True, False)
    line_step()
    wait_bytes(kv_slot(0), kv_recv.at[0])
    hand_over(2 + c, 3)
    wait_bytes(kv_slot(0), kv_recv.at[3])
    attend([2, 3], False, False)
    line_end()
    wait_bytes(kv_slot(0), kv_recv.at[1])
    pl.when(c == 1)(lambda: hand_over(1, 2))
    wait_bytes(kv_slot(0), kv_recv.at[2])
    attend([jnp.where(c == 0, 0, 4), 1], False, True)
    after_own()
    wait_bytes(fin.at[pl.ds(0, 20)], fin_recv)
    squares = jnp.zeros((128, HEAD_DIM), jnp.float32)
    for cs in (0, 1):
        for k in range(16):
            r, u = k // 4, k % 4
            lanes = slice((2 * k + cs) * 128, (2 * k + cs + 1) * 128)
            value = residual[:, lanes].astype(jnp.float32)
            for side in range(3):
                value = value + fin[
                    (side * 2 + cs) * 4 + r, :, u * 128 : (u + 1) * 128
                ].astype(jnp.float32)
            hidden[:, lanes] = value
            squares = squares + value * value
    variance = jnp.sum(squares, axis=1, keepdims=True) * (1.0 / D)
    shrink = lax.rsqrt(variance + 1e-06)
    for first in range(0, D, CHUNK):
        lanes = slice(first, first + CHUNK)
        normed[:, lanes] = (hidden[:, lanes] * shrink * gain[:, lanes]).astype(jnp.bfloat16)

    for _ in range(4):
        wait_bytes(kv_slot(0), kv_send)
    wait_bytes(weight.at[pl.ds(0, 15)], weight_send)
    wait_bytes(stage.at[pl.ds(0, 8)], att_send)
    wait_bytes(stage.at[pl.ds(0, 28)], term_send)


def front(queries, keys, values, doc_lengths, out_weight, residual, norm_gain):
    vmem = pl.BlockSpec(memory_space=pltpu.VMEM)
    dma = pltpu.SemaphoreType.DMA
    tokens = residual.shape[0]
    return pl.pallas_call(
        front_kernel,
        out_shape=(
            jax.ShapeDtypeStruct((tokens, D), jnp.bfloat16),
            jax.ShapeDtypeStruct((tokens, D), jnp.float32),
        ),
        in_specs=[pl.BlockSpec(memory_space=pltpu.SMEM)] + [vmem] * 6,
        out_specs=(vmem, vmem),
        scratch_shapes=[
            pltpu.VMEM((6 * SHARD, 2 * HEAD_DIM), jnp.bfloat16),
            pltpu.VMEM((16, 1024, HEAD_DIM), jnp.bfloat16),
            pltpu.VMEM((4, 2, 128, 1024), jnp.bfloat16),
            pltpu.VMEM((8, 128, 512), jnp.bfloat16),
            pltpu.VMEM((32, 128, 512), jnp.bfloat16),
            pltpu.VMEM((24, 128, 512), jnp.bfloat16),
            pltpu.VMEM((16, 256, 128), jnp.float32),
            pltpu.VMEM((16, 256, 128), jnp.float32),
            pltpu.VMEM((16, 256, 128), jnp.float32),
            dma, dma((4,)), dma((2,)), dma((2,)), dma((2,)), dma((2,)), dma,
            dma, dma((4,)), dma((4,)), dma, dma,
        ],
        compiler_params=pltpu.CompilerParams(
            has_side_effects=True, vmem_limit_bytes=60 * 1024 * 1024, collective_id=1
        ),
        cost_estimate=pl.CostEstimate(
            flops=10**10, bytes_accessed=10**7, transcendentals=10**7
        ),
    )(doc_lengths, queries, keys, values, out_weight, residual, norm_gain.reshape(1, D))


def body(
    queries, keys, values, doc_lengths, out_weight, residual, norm_gain, expert_ids,
    gate_values, w_gate, w_up, w_down,
):
    normed, hidden = front(queries, keys, values, doc_lengths, out_weight, residual, norm_gain)
    return routed_layer(normed, hidden, expert_ids, gate_values, w_gate, w_up, w_down)


def solution(mesh):
    in_specs = (
        P("seq", "exp"),
        P("seq", "exp"),
        P("seq", "exp"),
        P(),
        P("exp", "seq"),
        P(("seq", "exp"), None),
        P(),
        P(("seq", "exp"), None),
        P(("seq", "exp"), None),
        P(("seq", "exp"), None, None),
        P(("seq", "exp"), None, None),
        P(("seq", "exp"), None, None),
    )
    out_specs = P(("seq", "exp"), None)
    return jax.shard_map(body, mesh=mesh, in_specs=in_specs, out_specs=out_specs, check_vma=False)
```

time: 347 us -> 333 us (0.960)
  Pallas kernels: 332 us -> 326 us
  other arithmetic: 5.35 us -> 0 us
    pallas_call x1, Pallas kernels: 94 us -> 82.2 us  [front(): pl.pallas_call(front_kernel, out_shape=(jax.ShapeDtypeStruct((tokens, D),...]
    pallas_call x1, Pallas kernels: 238 us -> 244 us  [routed_layer(): pl.pallas_call(moe_kernel, out_shape=jax.ShapeDtypeStruct((tokens, D), jn...]
where the time goes in v3:
time: 333 us; the launch traced here: 328 us
  Pallas kernels  326 us (98%)
    pallas_call x1, Pallas kernels, routed_layer(): pl.pallas_call(moe_kernel, out_shape=jax.ShapeDtypeStruct((tokens, D), jn...  244 us
    pallas_call x1, Pallas kernels, front(): pl.pallas_call(front_kernel, out_shape=(jax.ShapeDtypeStruct((tokens, D),...  82.2 us

profile of v3, /device:TPU:38, one launch (start us, length us, event | category | flops | bytes accessed | tf_op | source)
XLA Modules:
  0.0 328.1 jit_solution(7622952261205382599)
XLA Ops:
  0.0 82.2 %shard_map.118 = (bf16[128,4096]{1,0:T(8,128)(2,1)}, f32[128,4096]{1,0:T(8,128)}) custom-call(s32[16]{0:T(128)} %doc_lengths.1, bf16[512,1024]{1,0:T(8,128)(2,1)} %queries.1, bf16[512,128]{1,0:T(8,128)(2,1)} %keys.1, bf16[512,128]{1,0:T(8,128)(2,1)} %values.1, bf16[1024,128]{1,0:T(8,128)(2,1)} %out_weight.1, bf16[128,4096]{1,0:T(8,128)(2,1)} %residual.1, ...), custom_call_target="tpu_custom_call" | custom-call | flops 10000000000 | bytes 10000000 | tf_op jit(solution)/shard_map/pallas_call | solution.py:602
  82.2 243.6 %shard_map.119 = bf16[128,4096]{1,0:T(8,128)(2,1)} custom-call(bf16[128,4096]{1,0:T(8,128)(2,1)} %get-tuple-element.7.normed, f32[128,4096]{1,0:T(8,128)} %get-tuple-element.8.hidden, s32[8,128]{1,0:T(8,128)} %bitcast.4, f32[8,128]{1,0:T(8,128)} %bitcast.5, bf16[1,4096,768]{2,1,0:T(8,128)(2,1)} %w_gate.1, bf16[1,4096,768]{2,1,0:T(8,128)(2,1)} %w_up.1, ...), custom_call_target="tpu_custom_call" | custom-call | flops 24000000000 | bytes 40000000 | tf_op jit(solution)/shard_map/pallas_call | solution.py:279
  325.8 2.3 copy.14

commit v4 on v3

--- a/solution.py
+++ b/solution.py
@@ -9,6 +9,7 @@
 
 HEAD_DIM = 128
 SHARD = 512
+BACK = 2048
 NEG_FILL = -1e30
 D = 4096
 HALF = D // 2
@@ -23,7 +24,7 @@
 EXTRA = D // 16
 MESSAGE = HALF + EXTRA
 CHUNK = 512
-STRIDE = 37
+STRIDE = 13
 MESH = pl.DeviceIdType.MESH
 
 
@@ -36,36 +37,61 @@
     return {"seq": (y * 4 + x) * 2 + c, "exp": z}
 
 
-def route_target(index):
+def line_axis(c, kind):
+    even = jnp.where(kind == 3, 2, kind)
+    odd = jnp.where(kind == 0, 2, jnp.where(kind == 3, 1, 0))
+    return jnp.where(c == 0, even, odd)
+
+
+def job_step(q):
+    return jnp.where(q == 2, 3, jnp.where(q == 3, 2, q))
+
+
+def along(axis, by):
+    return jnp.where(axis == 1, by, 0), jnp.where(axis == 0, by, 0), jnp.where(axis == 2, by, 0)
+
+
+def across(axis, d1, d2):
+    ey = jnp.where(axis == 0, d1, jnp.where(axis == 1, 0, d2))
+    ex = jnp.where(axis == 0, 0, jnp.where(axis == 1, d2, d1))
+    ez = jnp.where(axis == 0, d2, jnp.where(axis == 1, d1, 0))
+    return ey, ex, ez
+
+
+def job_axis(q):
     y, x, c, z = place()
-    j = (index * STRIDE) % DEVICES
-    dy, dx, dc, dz = j // 32, (j // 8) % 4, (j // 4) % 2, j % 4
-    ey = jnp.where(c == 0, dy, dx)
-    ex = jnp.where(c == 0, dx, dz)
-    ez = jnp.where(c == 0, dz, dy)
-    return (y + ey) % 4, (x + ex) % 4, (c + dc) % 2, (z + ez) % 4
-
-
-def route_source(index):
+    return line_axis(c, (x + y + z + job_step(q)) % 4)
+
+
+def job_block(q):
     y, x, c, z = place()
-    j = (index * STRIDE) % DEVICES
-    dy, dx, dc, dz = j // 32, (j // 8) % 4, (j // 4) % 2, j % 4
-    sc = (c + dc) % 2
-    ey = jnp.where(sc == 0, dy, dx)
-    ex = jnp.where(sc == 0, dx, dz)
-    ez = jnp.where(sc == 0, dz, dy)
+    ey, ex, ez = along(job_axis(q), job_step(q))
+    return (y + ey) % 4, (x + ex) % 4, c, (z + ez) % 4
+
+
+def job_target(q, n):
+    y, x, c, z = place()
+    m = (n * STRIDE) % PER_GROUP
+    ey, ex, ez = across(job_axis(q), (m // 4) % 4, m % 4)
+    return (y + ey) % 4, (x + ex) % 4, (c + m // 16) % 2, (z + ez) % 4
+
+
+def job_source(q, n):
+    y, x, c, z = place()
+    m = (n * STRIDE) % PER_GROUP
+    d1, d2 = (m // 4) % 4, m % 4
+    sc = (c + m // 16) % 2
+    kind = (x + y + z - d1 - d2 + 8) % 4
+    ey, ex, ez = across(line_axis(sc, (kind + job_step(q)) % 4), d1, d2)
     return (y - ey + 4) % 4, (x - ex + 4) % 4, sc, (z - ez + 4) % 4
 
 
-def target_ids(first):
+def job_target_ids(q):
     y, x, c, z = place()
-    index = first + lax.broadcasted_iota(jnp.int32, (1, PER_GROUP), 1)
-    j = (index * STRIDE) & (DEVICES - 1)
-    dy, dx, dc, dz = j >> 5, (j >> 3) & 3, (j >> 2) & 1, j & 3
-    ey = jnp.where(c == 0, dy, dx)
-    ex = jnp.where(c == 0, dx, dz)
-    ez = jnp.where(c == 0, dz, dy)
-    ty, tx, tc, tz = (y + ey) & 3, (x + ex) & 3, (c + dc) & 1, (z + ez) & 3
+    n = lax.broadcasted_iota(jnp.int32, (1, PER_GROUP), 1)
+    m = (n * STRIDE) & (PER_GROUP - 1)
+    ey, ex, ez = across(job_axis(q), (m >> 2) & 3, m & 3)
+    ty, tx, tc, tz = (y + ey) & 3, (x + ex) & 3, (c + (m >> 4)) & 1, (z + ez) & 3
     return (((ty * 4 + tx) * 2 + tc) * 4 + tz).astype(jnp.float32)
 
 
@@ -75,18 +101,36 @@
 
 def moe_kernel(
     normed, hidden, ids_t, gates_t, w_gate, w_up, w_down, out,
-    outbound, arrived, returned, wg, wu, wd, rows, extra, acc, perm, posn, gate,
+    outbound, arrived, returned, wg, wu, wd, rows, extra, acc, perm, blocks, parts, meta, posn, gate,
     weight_sem, hidden_sem, send_sem, recv_sem, back_send_sem, back_recv_sem,
+    line_send, line_recv, part_send, part_recv,
 ):
     tokens = normed.shape[0]
+    y, x, c, z = place()
+    meta[0] = jnp.transpose(
+        jnp.concatenate(
+            [
+                ids_t[...].astype(jnp.float32), gates_t[...],
+                jnp.zeros((tokens - 2 * TOPK, tokens), jnp.float32),
+            ],
+            axis=0,
+        )
+    )
+    own_axis = line_axis(c, (x + y + z) % 4)
+    for q, step in ((1, 1), (2, 3), (3, 2)):
+        ey, ex, ez = along(own_axis, 4 - step)
+        target = device((y + ey) % 4, (x + ex) % 4, c, (z + ez) % 4)
+        for k, (src, dst) in enumerate(((meta.at[0], meta.at[q]), (normed, blocks.at[q - 1]))):
+            pltpu.make_async_remote_copy(
+                src_ref=src, dst_ref=dst, send_sem=line_send.at[k], recv_sem=line_recv.at[q - 1, k],
+                device_id=target, device_id_type=MESH,
+            ).start()
     loads = [
         pltpu.make_async_copy(src.at[0], dst, weight_sem.at[k])
         for k, (src, dst) in enumerate(((w_gate, wg), (w_up, wu), (w_down, wd)))
     ]
     for load in loads:
         load.start()
-    fetch = pltpu.make_async_copy(hidden, acc, hidden_sem)
-    fetch.start()
     line = lax.broadcasted_iota(jnp.int32, (16 * PER_GROUP, 16 * PER_GROUP), 0)
     other = lax.broadcasted_iota(jnp.int32, (16 * PER_GROUP, 16 * PER_GROUP), 1)
     perm[...] = (other == (line & (PER_GROUP - 1)) * 16 + (line >> 5)).astype(jnp.bfloat16)
@@ -122,29 +166,20 @@
                 j * PER_GROUP : (j + 1) * PER_GROUP
             ].astype(jnp.bfloat16)
 
-    routes = jnp.transpose(
-        jnp.concatenate(
-            [
-                ids_t[...].astype(jnp.float32), gates_t[...],
-                jnp.zeros((tokens - 2 * TOPK, tokens), jnp.float32),
-            ],
-            axis=0,
-        )
-    )
     earlier = (
         lax.broadcasted_iota(jnp.int32, (tokens, tokens), 0)
         > lax.broadcasted_iota(jnp.int32, (tokens, tokens), 1)
     ).astype(jnp.bfloat16)
 
-    def build(q, carry):
+    def build(q, source):
         first = q * PER_GROUP
-        target = target_ids(first)
+        target = job_target_ids(q)
         member = jnp.zeros((tokens, PER_GROUP), jnp.float32)
         weight = jnp.zeros((tokens, PER_GROUP), jnp.float32)
         for k in range(TOPK):
-            hit = routes[:, k : k + 1] == target
+            hit = meta[q, :, k : k + 1] == target
             member = jnp.where(hit, 1.0, member)
-            weight = jnp.where(hit, routes[:, TOPK + k : TOPK + k + 1], weight)
+            weight = jnp.where(hit, meta[q, :, TOPK + k : TOPK + k + 1], weight)
         count = jnp.dot(earlier, member.astype(jnp.bfloat16), preferred_element_type=jnp.float32)
         count = jnp.where(member > 0.0, count, -1.0)
         posn[q] = count
@@ -164,40 +199,41 @@
             halves = []
             for base in (c, HALF + c):
                 got = jnp.dot(
-                    picks, normed[:, base : base + CHUNK], preferred_element_type=jnp.float32
+                    picks, source[:, base : base + CHUNK], preferred_element_type=jnp.float32
                 )
                 extra[:, base : base + CHUNK] = got[MAIN:ROWS]
                 halves.append(got[0:MAIN])
             pack(outbound, first, c, *halves)
         pack_extra(outbound, first)
-
-        def send(k, carry):
-            index = first + k
-
-            @pl.when(index == 0)
-            def _():
-                pltpu.make_async_copy(outbound.at[0], arrived.at[0], recv_sem.at[0]).start()
-
-            @pl.when(index > 0)
-            def _():
-                pltpu.make_async_remote_copy(
-                    src_ref=outbound.at[index],
-                    dst_ref=arrived.at[index],
-                    send_sem=send_sem,
-                    recv_sem=recv_sem.at[q],
-                    device_id=device(*route_target(index)),
-                    device_id_type=MESH,
-                ).start()
-
+        pltpu.make_async_copy(outbound.at[first], arrived.at[first], recv_sem.at[q]).start()
+
+        def send(n, carry):
+            pltpu.make_async_remote_copy(
+                src_ref=outbound.at[first + n],
+                dst_ref=arrived.at[first + n],
+                send_sem=send_sem,
+                recv_sem=recv_sem.at[q],
+                device_id=device(*job_target(q, n)),
+                device_id_type=MESH,
+            ).start()
             return carry
 
-        return lax.fori_loop(0, PER_GROUP, send, carry)
-
-    lax.fori_loop(0, GROUPS, build, 0)
+        lax.fori_loop(1, PER_GROUP, send, 0)
+
+    build(0, normed)
+
+    def build_other(q, carry):
+        for k, ref in enumerate((meta.at[0], normed)):
+            pltpu.make_async_copy(ref, ref, line_recv.at[q - 1, k]).wait()
+        build(q, blocks.at[q - 1])
+        return carry
+
+    lax.fori_loop(1, GROUPS, build_other, 0)
     for load in loads:
         load.wait()
 
-    def expert(q, carry):
+    def expert(i, carry):
+        q = (i + 1) % GROUPS
         first = q * PER_GROUP
         block = arrived.at[pl.ds(first, PER_GROUP)]
         pltpu.make_async_copy(block, block, recv_sem.at[q]).wait()
@@ -215,28 +251,20 @@
                 halves.append(got[0:MAIN])
             pack(arrived, first, c, *halves)
         pack_extra(arrived, first)
-
-        def send(k, carry):
-            index = first + k
-
-            @pl.when(index == 0)
-            def _():
-                pltpu.make_async_copy(arrived.at[0], returned.at[0], back_recv_sem.at[0]).start()
-
-            @pl.when(index > 0)
-            def _():
-                pltpu.make_async_remote_copy(
-                    src_ref=arrived.at[index],
-                    dst_ref=returned.at[index],
-                    send_sem=back_send_sem,
-                    recv_sem=back_recv_sem.at[q],
-                    device_id=device(*route_source(index)),
-                    device_id_type=MESH,
-                ).start()
-
+        pltpu.make_async_copy(arrived.at[first], returned.at[first], back_recv_sem.at[q]).start()
+
+        def send(n, carry):
+            pltpu.make_async_remote_copy(
+                src_ref=arrived.at[first + n],
+                dst_ref=returned.at[first + n],
+                send_sem=back_send_sem,
+                recv_sem=back_recv_sem.at[q],
+                device_id=device(*job_source(q, n)),
+                device_id_type=MESH,
+            ).start()
             return carry
 
-        return lax.fori_loop(0, PER_GROUP, send, carry)
+        return lax.fori_loop(1, PER_GROUP, send, carry)
 
     lax.fori_loop(0, GROUPS, expert, 0)
     row = lax.broadcasted_iota(jnp.int32, (PER_GROUP, ROWS), 1)
@@ -245,7 +273,7 @@
     _, slot = slot_of(lax.broadcasted_iota(jnp.int32, (tokens, ROWS), 1))
     slot = slot.astype(jnp.float32)
 
-    def combine(q, carry):
+    def combine(q):
         first = q * PER_GROUP
         block = returned.at[pl.ds(first, PER_GROUP)]
         pltpu.make_async_copy(block, block, back_recv_sem.at[q]).wait()
@@ -259,13 +287,30 @@
         ).astype(jnp.bfloat16)
         for c in range(0, D, CHUNK):
             got = jnp.dot(both, rows[:, c : c + CHUNK], preferred_element_type=jnp.float32)
-            acc[:, c : c + CHUNK] += got[0:tokens] + got[tokens : 2 * tokens]
+            yield slice(c, c + CHUNK), got[0:tokens] + got[tokens : 2 * tokens]
+
+    def combine_other(q, carry):
+        for lanes, value in combine(q):
+            blocks[q - 1, :, lanes] = value.astype(jnp.bfloat16)
+        pltpu.make_async_remote_copy(
+            src_ref=blocks.at[q - 1], dst_ref=parts.at[q - 1], send_sem=part_send,
+            recv_sem=part_recv.at[q - 1], device_id=device(*job_block(q)), device_id_type=MESH,
+        ).start()
         return carry
 
+    lax.fori_loop(1, GROUPS, combine_other, 0)
+    fetch = pltpu.make_async_copy(hidden, acc, hidden_sem)
+    fetch.start()
     fetch.wait()
-    lax.fori_loop(0, GROUPS, combine, 0)
-    out[...] = acc[...].astype(jnp.bfloat16)
-    sent = outbound.at[pl.ds(1, DEVICES - 1)]
+    for q in range(1, GROUPS):
+        pltpu.make_async_copy(normed, normed, part_recv.at[q - 1]).wait()
+        acc[...] += parts[q - 1].astype(jnp.float32)
+    for lanes, value in combine(0):
+        out[:, lanes] = (acc[:, lanes] + value).astype(jnp.bfloat16)
+    for k, ref in enumerate((meta.at[pl.ds(0, 3)], blocks)):
+        pltpu.make_async_copy(ref, ref, line_send.at[k]).wait()
+    pltpu.make_async_copy(blocks, blocks, part_send).wait()
+    sent = outbound.at[pl.ds(0, DEVICES - GROUPS)]
     for sem in (send_sem, back_send_sem):
         pltpu.make_async_copy(sent, sent, sem).wait()
 
@@ -290,9 +335,13 @@
             pltpu.VMEM((PER_GROUP, D), jnp.float32),
             pltpu.VMEM((tokens, D), jnp.float32),
             pltpu.VMEM((16 * PER_GROUP, 16 * PER_GROUP), jnp.bfloat16),
+            pltpu.VMEM((GROUPS - 1, tokens, D), jnp.bfloat16),
+            pltpu.VMEM((GROUPS - 1, tokens, D), jnp.bfloat16),
+            pltpu.VMEM((GROUPS, tokens, 128), jnp.float32),
             pltpu.VMEM((GROUPS, tokens, PER_GROUP), jnp.float32),
             pltpu.VMEM((GROUPS, tokens, PER_GROUP), jnp.float32),
             dma((3,)), dma, dma, dma((GROUPS,)), dma, dma((GROUPS,)),
+            dma((2,)), dma((GROUPS - 1, 2)), dma, dma((GROUPS - 1,)),
         ],
         compiler_params=pltpu.CompilerParams(
             has_side_effects=True, vmem_limit_bytes=64 * 1024 * 1024

time: 333 us -> 308 us (0.925); the launches traced: 328 us -> 307 us
  Pallas kernels: 326 us -> 305 us
    pallas_call x1, Pallas kernels: 244 us -> 223 us  [routed_layer(): pl.pallas_call(moe_kernel, out_shape=jax.ShapeDtypeStruct((tokens, D), jn...]
where the time goes in v4:
time: 308 us; the launch traced here: 307 us
  Pallas kernels  305 us (99%)
    pallas_call x1, Pallas kernels, routed_layer(): pl.pallas_call(moe_kernel, out_shape=jax.ShapeDtypeStruct((tokens, D), jn...  223 us
    pallas_call x1, Pallas kernels, front(): pl.pallas_call(front_kernel, out_shape=(jax.ShapeDtypeStruct((tokens, D),...  82.2 us

profile of v4, /device:TPU:38, one launch (start us, length us, event | category | flops | bytes accessed | tf_op | source)
XLA Modules:
  0.0 307.3 jit_solution(9940172068455204685)
XLA Ops:
  0.0 82.2 %shard_map.118 = (bf16[128,4096]{1,0:T(8,128)(2,1)}, f32[128,4096]{1,0:T(8,128)}) custom-call(s32[16]{0:T(128)} %doc_lengths.1, bf16[512,1024]{1,0:T(8,128)(2,1)} %queries.1, bf16[512,128]{1,0:T(8,128)(2,1)} %keys.1, bf16[512,128]{1,0:T(8,128)(2,1)} %values.1, bf16[1024,128]{1,0:T(8,128)(2,1)} %out_weight.1, bf16[128,4096]{1,0:T(8,128)(2,1)} %residual.1, ...), custom_call_target="tpu_custom_call" | custom-call | flops 10000000000 | bytes 10000000 | tf_op jit(solution)/shard_map/pallas_call | solution.py:651
  82.2 222.8 %shard_map.119 = bf16[128,4096]{1,0:T(8,128)(2,1)} custom-call(bf16[128,4096]{1,0:T(8,128)(2,1)} %get-tuple-element.7.normed, f32[128,4096]{1,0:T(8,128)} %get-tuple-element.8.hidden, s32[8,128]{1,0:T(8,128)} %bitcast.4, f32[8,128]{1,0:T(8,128)} %bitcast.5, bf16[1,4096,768]{2,1,0:T(8,128)(2,1)} %w_gate.1, bf16[1,4096,768]{2,1,0:T(8,128)(2,1)} %w_up.1, ...), custom_call_target="tpu_custom_call" | custom-call | flops 24000000000 | bytes 40000000 | tf_op jit(solution)/shard_map/pallas_call | solution.py:324
  305.0 2.3 copy.14

commit v5 on v4

--- a/solution.py
+++ b/solution.py
@@ -302,11 +302,16 @@
     fetch = pltpu.make_async_copy(hidden, acc, hidden_sem)
     fetch.start()
     fetch.wait()
+    for lanes, value in combine(0):
+        acc[:, lanes] += value
     for q in range(1, GROUPS):
         pltpu.make_async_copy(normed, normed, part_recv.at[q - 1]).wait()
-        acc[...] += parts[q - 1].astype(jnp.float32)
-    for lanes, value in combine(0):
-        out[:, lanes] = (acc[:, lanes] + value).astype(jnp.bfloat16)
+    for c in range(0, D, CHUNK):
+        lanes = slice(c, c + CHUNK)
+        value = acc[:, lanes]
+        for q in range(1, GROUPS):
+            value = value + parts[q - 1, :, lanes].astype(jnp.float32)
+        out[:, lanes] = value.astype(jnp.bfloat16)
     for k, ref in enumerate((meta.at[pl.ds(0, 3)], blocks)):
         pltpu.make_async_copy(ref, ref, line_send.at[k]).wait()
     pltpu.make_async_copy(blocks, blocks, part_send).wait()
@@ -396,6 +401,18 @@
     def kv_slot(slot):
         return kv.at[pl.ds(pl.multiple_of(slot * SHARD, SHARD), SHARD)]
 
+    own = pl.ds(pl.multiple_of((4 + c) * SHARD, SHARD), SHARD)
+    kv[own, 0:HEAD_DIM] = keys[...]
+    kv[own, HEAD_DIM : 2 * HEAD_DIM] = values[...]
+
+    def send_kv(ahead):
+        remote(
+            kv_slot(4 + c), kv_slot(4 - 2 * ahead + c), kv_send, kv_recv.at[ahead - 1],
+            chip_device(rotated(chip, ahead), c, z),
+        ).start()
+
+    send_kv(1)
+
     weight[chip] = out_weight[...]
 
     def spread(u):
@@ -411,14 +428,7 @@
             block, block, weight_send, line_recv.at[way], device(y, (x + step) % 4, c, z)
         ).start()
     spread(x)
-    own = pl.ds(pl.multiple_of((4 + c) * SHARD, SHARD), SHARD)
-    kv[own, 0:HEAD_DIM] = keys[...]
-    kv[own, HEAD_DIM : 2 * HEAD_DIM] = values[...]
-    for ahead in (1, 2):
-        remote(
-            kv_slot(4 + c), kv_slot(4 - 2 * ahead + c), kv_send, kv_recv.at[ahead - 1],
-            chip_device(rotated(chip, ahead), c, z),
-        ).start()
+    send_kv(2)
 
     def line_step():
         for way, step in enumerate((1, 3)):

time: 308 us -> 306 us (level)
  no operation moved by 1% of the time
where the time goes in v5:
time: 306 us
  Pallas kernels  303 us (99%)
    pallas_call x1, Pallas kernels, routed_layer(): pl.pallas_call(moe_kernel, out_shape=jax.ShapeDtypeStruct((tokens, D), jn...  221 us
    pallas_call x1, Pallas kernels, front(): pl.pallas_call(front_kernel, out_shape=(jax.ShapeDtypeStruct((tokens, D),...  81.9 us

profile of v5, /device:TPU:38, one launch (start us, length us, event | category | flops | bytes accessed | tf_op | source)
XLA Modules:
  0.0 305.6 jit_solution(5213686839572341308)
XLA Ops:
  0.0 81.9 %shard_map.118 = (bf16[128,4096]{1,0:T(8,128)(2,1)}, f32[128,4096]{1,0:T(8,128)}) custom-call(s32[16]{0:T(128)} %doc_lengths.1, bf16[512,1024]{1,0:T(8,128)(2,1)} %queries.1, bf16[512,128]{1,0:T(8,128)(2,1)} %keys.1, bf16[512,128]{1,0:T(8,128)(2,1)} %values.1, bf16[1024,128]{1,0:T(8,128)(2,1)} %out_weight.1, bf16[128,4096]{1,0:T(8,128)(2,1)} %residual.1, ...), custom_call_target="tpu_custom_call" | custom-call | flops 10000000000 | bytes 10000000 | tf_op jit(solution)/shard_map/pallas_call | solution.py:661
  81.9 221.4 %shard_map.119 = bf16[128,4096]{1,0:T(8,128)(2,1)} custom-call(bf16[128,4096]{1,0:T(8,128)(2,1)} %get-tuple-element.7.normed, f32[128,4096]{1,0:T(8,128)} %get-tuple-element.8.hidden, s32[8,128]{1,0:T(8,128)} %bitcast.4, f32[8,128]{1,0:T(8,128)} %bitcast.5, bf16[1,4096,768]{2,1,0:T(8,128)(2,1)} %w_gate.1, bf16[1,4096,768]{2,1,0:T(8,128)(2,1)} %w_up.1, ...), custom_call_target="tpu_custom_call" | custom-call | flops 24000000000 | bytes 40000000 | tf_op jit(solution)/shard_map/pallas_call | solution.py:329
  303.3 2.3 copy.14
